TPU v7x, 256 devices: a whole 4x4x8 slice. The times are simulated.
256 devices in a mesh: tm: 8 (over y, core), chan: 32 (over x, z).
Axes of the slice: x: 4, y: 4, z: 8, core: 2. Of those that a mesh axis runs over, the one named last changes fastest.
Arguments:
- records: bfloat16 [24, 5120, 3000], P('tm', 'chan'), may hold values from -6 to 6
- partner: int32 [32, 7], P('chan'), may hold values from 0 to 31, as said below
- valid: int32 [32, 7], P('chan'), may hold values from 0 to 1
Outputs:
- stacked: bfloat16 [2, 32, 35840, 160], P(None, 'tm', 'chan')
Inputs may be any that keep to these rules, and one draw needn't show every extreme that they name: Each partner lies within 3 of its row's block index; the valid partners of a row are distinct, and padded slots name the row's own block.
All inputs are finite; a program needn't handle non-finite values.
Results may differ from a plain program's by a relative error of at most 0.0066.
Values may be sent and summed in bfloat16 or wider, within the bound.
No kernel may reach another device: no remote copies, remote signals or barrier semaphores. Data moves between devices by JAX's collectives and lax.ppermute only.
A program may use at most 64 MiB of HBM per device.

v0:
```python
import math

import jax
import jax.numpy as jnp
from jax import lax
from jax.sharding import PartitionSpec as P

BINS = 32
REACH = 3


def shifted(block, axis, distance):
    devices = range(lax.axis_size(axis))
    route = [(i - distance, i) for i in devices if i - distance in devices]
    return lax.ppermute(block, axis, route)


def spectra_table(length, bins):
    times = lax.iota(jnp.int32, length)
    freqs = 60 + 10 * lax.iota(jnp.int32, bins)
    phase = freqs[:, None] * times[None, :] % length
    angle = phase.astype(jnp.float32) * (2.0 * math.pi / length)
    return jnp.concatenate([jnp.cos(angle), -jnp.sin(angle)], 0).astype(jnp.bfloat16)


def per_device(records, partner, valid):
    seg_local, width, length = records.shape
    bins = BINS
    table = spectra_table(length, bins)
    spectrum = jnp.einsum("kl,scl->skc", table, records, preferred_element_type=jnp.float32)
    power = jnp.mean(spectrum * spectrum, axis=1, keepdims=True)
    white = (spectrum * lax.rsqrt(power + 1e-06)).astype(jnp.bfloat16)
    white = white.reshape(seg_local, 2, bins, width)
    regrouped = lax.all_to_all(white, "tm", split_axis=2, concat_axis=0, tiled=True)
    seg_all, _, bins_local, _ = regrouped.shape
    slots = partner.shape[1]
    neighbours = []
    for offset in range(-REACH, REACH + 1):
        if offset == 0:
            neighbours.append(regrouped)
        else:
            neighbours.append(shifted(regrouped, "chan", -offset))
    stacked_near = jnp.stack(neighbours, 0).reshape(2 * REACH + 1, -1)
    relative = partner[0] - lax.axis_index("chan") + REACH
    selector = (relative[:, None] == lax.iota(jnp.int32, 2 * REACH + 1)[None, :]).astype(
        jnp.bfloat16
    )
    picked = jnp.dot(selector, stacked_near, preferred_element_type=jnp.float32).astype(
        jnp.bfloat16
    )
    others = picked.reshape(slots, seg_all, 2, bins_local, width)
    own_cat = jnp.transpose(regrouped, (2, 1, 0, 3)).reshape(bins_local, 2 * seg_all, width)
    swapped = jnp.stack([regrouped[:, 1], -regrouped[:, 0]], 1)
    own_swap = jnp.transpose(swapped, (2, 1, 0, 3)).reshape(bins_local, 2 * seg_all, width)
    other_cat = jnp.transpose(others, (0, 3, 2, 1, 4)).reshape(
        slots, bins_local, 2 * seg_all, width
    )
    real_part = jnp.einsum("fka,pfkb->fpab", own_cat, other_cat, preferred_element_type=jnp.float32)
    imag_part = jnp.einsum(
        "fka,pfkb->fpab", own_swap, other_cat, preferred_element_type=jnp.float32
    )
    weight = valid[0].astype(jnp.float32).reshape(1, slots, 1, 1) * (1.0 / math.sqrt(seg_all))
    result = jnp.stack([real_part * weight, imag_part * weight], 0).astype(jnp.bfloat16)
    return result.reshape(2, bins_local, slots * width, width)


def solution(mesh):
    return jax.shard_map(
        per_device,
        mesh=mesh,
        in_specs=(P("tm", "chan", None), P("chan", None), P("chan", None)),
        out_specs=P(None, "tm", "chan", None),
        check_vma=False,
    )
```

profile of v0, /device:TPU:6, one launch (start us, length us, event | category | flops | bytes accessed | tf_op | source)
XLA Modules:
  0.0 77.9 jit_solution(6927750007332762225)
XLA Ops:
  0.0 0.0 copy-start
  0.0 0.0 copy-start.2
  0.0 0.0 copy-start.3
  0.0 1.8 %cosine_convert_fusion = (bf16[32,3000]{1,0:T(8,128)(2,1)S(1)}, bf16[32,3000]{1,0:T(8,128)(2,1)S(1)}) fusion(s32[32]{0:T(128)S(1)} %multiply_add_fusion), kind=kLoop, calls=%fused_computation.12 | loop fusion | flops 1152000 | bytes 384128 | tf_op jit(solution)/shard_map/convert.6
  1.8 0.0 copy-done
  1.8 1.1 %multiply_reduce_fusion = (f32[3,160]{1,0:T(4,128)S(1)}, f32[64,3,160]{2,0,1:T(8,128)S(1)}) fusion(bf16[3,160,3000]{2,1,0:T(8,128)(2,1)S(1)} %copy-done, bf16[32,3000]{1,0:T(8,128)(2,1)S(1)} %get-tuple-element.8, bf16[32,3000]{1,0:T(8,128)(2,1)S(1)} %get-tuple-element.7), kind=kOutput, calls=%fused_computation.18 | convolution fusion | flops 185148960 | bytes 3388800 | tf_op jit(solution)/shard_map/kl,scl->skc/dot_general | solution.py:30
  3.0 0.7 copy.21
  3.7 4.5 %all-to-all-start = ((bf16[3,2,32,160]{3,1,0,2:T(2,128)(2,1)}), bf16[3,2,32,160]{3,1,0,2:T(2,128)(2,1)S(1)}, u32[]{:S(2)}, u32[]{:S(2)}) async-start(bf16[3,2,32,160]{3,1,0,2:T(2,128)(2,1)} %copy.21), calls=%async_computation | async-start | bytes 196608 | tf_op jit(solution)/shard_map/all_to_all | solution.py:34
  8.2 0.0 copy-done.2
  8.2 0.0 copy-done.3
  8.2 5.8 %all-to-all-done = bf16[3,2,32,160]{3,1,0,2:T(2,128)(2,1)S(1)} async-done(((bf16[3,2,32,160]{3,1,0,2:T(2,128)(2,1)}), bf16[3,2,32,160]{3,1,0,2:T(2,128)(2,1)S(1)}, u32[]{:S(2)}, u32[]{:S(2)}) %all-to-all-start) | async-done | bytes 61472 | tf_op jit(solution)/shard_map/all_to_all | solution.py:34
  14.0 8.9 %collective-permute-start.5 = (bf16[24,2,4,160]{3,2,1,0:T(4,128)(2,1)S(1)}, bf16[24,2,4,160]{3,2,1,0:T(4,128)(2,1)S(1)}, u32[]{:S(2)}, u32[]{:S(2)}) collective-permute-start(bf16[24,2,4,160]{3,2,1,0:T(4,128)(2,1)S(1)} %bitcast.51), channel_id=1, source_target_pairs={{3,0},{4,1},{5,2},{6,3},{7,4},{8,5},{9,6},{10,7},{11,8},{12,9},{13... | collective-permute-start | bytes 184328 | tf_op jit(solution)/shard_map/ppermute | solution.py:15
  23.0 2.5 %collective-permute-start.4 = (bf16[24,2,4,160]{3,2,1,0:T(4,128)(2,1)S(1)}, bf16[24,2,4,160]{3,2,1,0:T(4,128)(2,1)}, u32[]{:S(2)}, u32[]{:S(2)}) collective-permute-start(bf16[24,2,4,160]{3,2,1,0:T(4,128)(2,1)S(1)} %bitcast.53), channel_id=1, source_target_pairs={{2,0},{3,1},{4,2},{5,3},{6,4},{7,5},{8,6},{9,7},{10,8},{11,9},{12,... | collective-permute-start | bytes 184328 | tf_op jit(solution)/shard_map/ppermute | solution.py:15
  25.5 2.4 %collective-permute-start.3 = (bf16[24,2,4,160]{3,2,1,0:T(4,128)(2,1)S(1)}, bf16[24,2,4,160]{3,2,1,0:T(4,128)(2,1)}, u32[]{:S(2)}, u32[]{:S(2)}) collective-permute-start(bf16[24,2,4,160]{3,2,1,0:T(4,128)(2,1)S(1)} %bitcast.54), channel_id=1, source_target_pairs={{1,0},{2,1},{3,2},{4,3},{5,4},{6,5},{7,6},{8,7},{9,8},{10,9},{11,1... | collective-permute-start | bytes 184328 | tf_op jit(solution)/shard_map/ppermute | solution.py:15
  27.9 3.5 %collective-permute-start.2 = (bf16[24,2,4,160]{3,2,1,0:T(4,128)(2,1)S(1)}, bf16[24,2,4,160]{3,2,1,0:T(4,128)(2,1)}, u32[]{:S(2)}, u32[]{:S(2)}) collective-permute-start(bf16[24,2,4,160]{3,2,1,0:T(4,128)(2,1)S(1)} %bitcast.55), channel_id=1, source_target_pairs={{0,1},{1,2},{2,3},{3,4},{4,5},{5,6},{6,7},{7,8},{8,9},{9,10},{10,1... | collective-permute-start | bytes 184328 | tf_op jit(solution)/shard_map/ppermute | solution.py:15
  31.4 4.3 %collective-permute-start.1 = (bf16[24,2,4,160]{3,2,1,0:T(4,128)(2,1)S(1)}, bf16[24,2,4,160]{3,2,1,0:T(4,128)(2,1)S(1)}, u32[]{:S(2)}, u32[]{:S(2)}) collective-permute-start(bf16[24,2,4,160]{3,2,1,0:T(4,128)(2,1)S(1)} %bitcast.56), channel_id=1, source_target_pairs={{0,2},{1,3},{2,4},{3,5},{4,6},{5,7},{6,8},{7,9},{8,10},{9,11},{10,... | collective-permute-start | bytes 184328 | tf_op jit(solution)/shard_map/ppermute | solution.py:15
  35.6 0.8 %stack.40 = bf16[1,30720]{1,0:T(2,128)(2,1)} reshape(bf16[8,3,2,4,160]{4,3,2,1,0:T(4,128)(2,1)S(1)} %copy.23) | data formatting | bytes 122880 | tf_op jit(solution)/shard_map/stack | solution.py:43
  36.5 0.0 collective-permute-done.5
  36.5 4.0 %collective-permute-start = (bf16[24,2,4,160]{3,2,1,0:T(4,128)(2,1)S(1)}, bf16[24,2,4,160]{3,2,1,0:T(4,128)(2,1)}, u32[]{:S(2)}, u32[]{:S(2)}) collective-permute-start(bf16[24,2,4,160]{3,2,1,0:T(4,128)(2,1)S(1)} %bitcast.58), channel_id=1, source_target_pairs={{0,3},{1,4},{2,5},{3,6},{4,7},{5,8},{6,9},{7,10},{8,11},{9,12},{10... | collective-permute-start | bytes 184328 | tf_op jit(solution)/shard_map/ppermute | solution.py:15
  40.5 0.1 maximum_bitcast_fusion.2
  40.6 0.7 copy.27
  41.3 0.8 %stack.43 = bf16[1,30720]{1,0:T(2,128)(2,1)} reshape(bf16[24,2,4,160]{3,2,1,0:T(4,128)(2,1)S(1)} %collective-permute-done.5) | data formatting | bytes 122880 | tf_op jit(solution)/shard_map/stack | solution.py:43
  42.1 0.0 collective-permute-done.4
  42.1 1.7 %stack.42 = bf16[1,30720]{1,0:T(2,128)(2,1)} reshape(bf16[24,2,4,160]{3,2,1,0:T(4,128)(2,1)} %collective-permute-done.4) | data formatting | bytes 122880 | tf_op jit(solution)/shard_map/stack | solution.py:43
  43.7 0.0 collective-permute-done.3
  43.8 1.7 %stack.41 = bf16[1,30720]{1,0:T(2,128)(2,1)} reshape(bf16[24,2,4,160]{3,2,1,0:T(4,128)(2,1)} %collective-permute-done.3) | data formatting | bytes 122880 | tf_op jit(solution)/shard_map/stack | solution.py:43
  45.4 0.0 collective-permute-done.2
  45.4 1.7 %stack.39 = bf16[1,30720]{1,0:T(2,128)(2,1)} reshape(bf16[24,2,4,160]{3,2,1,0:T(4,128)(2,1)} %collective-permute-done.2) | data formatting | bytes 122880 | tf_op jit(solution)/shard_map/stack | solution.py:43
  47.1 0.0 collective-permute-done.1
  47.1 0.8 %stack.38 = bf16[1,30720]{1,0:T(2,128)(2,1)} reshape(bf16[24,2,4,160]{3,2,1,0:T(4,128)(2,1)S(1)} %collective-permute-done.1) | data formatting | bytes 122880 | tf_op jit(solution)/shard_map/stack | solution.py:43
  47.9 1.7 %collective-permute-done = bf16[24,2,4,160]{3,2,1,0:T(4,128)(2,1)} collective-permute-done((bf16[24,2,4,160]{3,2,1,0:T(4,128)(2,1)S(1)}, bf16[24,2,4,160]{3,2,1,0:T(4,128)(2,1)}, u32[]{:S(2)}, u32[]{:S(2)}) %collective-permute-start) | collective-permute-done | bytes 61472 | tf_op jit(solution)/shard_map/ppermute | solution.py:15
  49.6 1.7 %stack.37 = bf16[1,30720]{1,0:T(2,128)(2,1)} reshape(bf16[24,2,4,160]{3,2,1,0:T(4,128)(2,1)} %collective-permute-done) | data formatting | bytes 122880 | tf_op jit(solution)/shard_map/stack | solution.py:43
  51.3 2.7 %stack.44 = bf16[7,30720]{1,0:T(8,128)(2,1)S(1)} concatenate(bf16[1,30720]{1,0:T(2,128)(2,1)} %stack.37, bf16[1,30720]{1,0:T(2,128)(2,1)} %stack.38, bf16[1,30720]{1,0:T(2,128)(2,1)} %stack.39, bf16[1,30720]{1,0:T(2,128)(2,1)} %stack.40, bf16[1,30720]{1,0:T(2,128)(2,1)} %stack.41, bf16[1,30720]{1,0:T(2,128)(2,1)} %stack.42, bf16[1,30720]{1,0:T(2,128)(2,1)} %stack.43), dimensions={0} | concatenate | bytes 860160 | tf_op jit(solution)/shard_map/stack | solution.py:43
  53.9 1.1 %convolution_convert_fusion = bf16[7,30720]{1,0:T(8,128)(2,1)} fusion(bf16[7,30720]{1,0:T(8,128)(2,1)S(1)} %stack.44, s32[7]{0:T(128)S(1)} %add_bitcast_fusion), kind=kOutput, calls=%fused_computation | convolution fusion | flops 3225649 | bytes 860188 | tf_op jit(solution)/shard_map/dot_general | solution.py:48
  55.1 2.6 %reshape.73 = bf16[7,24,2,4,160]{4,3,2,1,0:T(4,128)(2,1)} reshape(bf16[7,30720]{1,0:T(8,128)(2,1)} %convolution_convert_fusion) | data formatting | bytes 860160 | tf_op jit(solution)/shard_map/reshape | solution.py:51
  57.7 1.2 %copy.25 = bf16[7,4,2,24,160]{4,3,2,0,1:T(8,128)(2,1)S(1)} copy(bf16[7,4,2,24,160]{4,1,2,3,0:T(4,128)(2,1)} %bitcast.50) | data formatting | bytes 860160 | tf_op jit(solution)/shard_map/transpose | solution.py:55
  58.9 0.0 copy-start.1
  58.9 0.9 %copy-done.1 = bf16[7,4,2,24,160]{4,3,2,0,1:T(8,128)(2,1)} copy-done((bf16[7,4,2,24,160]{4,3,2,0,1:T(8,128)(2,1)}, bf16[7,4,2,24,160]{4,3,2,0,1:T(8,128)(2,1)S(1)}, u32[]{:S(2)}) %copy-start.1) | copy-done | bytes 430104
  59.8 3.1 %multiply_convert_fusion = bf16[4,7,160,160]{2,3,1,0:T(8,128)(2,1)} fusion(f32[7]{0:T(128)S(1)} %multiply_bitcast_fusion, bf16[7,4,48,160]{3,2,0,1:T(8,128)(2,1)S(1)} %bitcast.48, bf16[4,48,160,1]{2,1,3,0:T(8,128)(2,1)} %bitcast.60), kind=kOutput, calls=%fused_computation.1 | convolution fusion | flops 70246400 | bytes 1925148 | tf_op jit(solution)/shard_map/fka,pfkb->fpab/dot_general | solution.py:59
  62.9 4.0 %copy.29 = bf16[1,4,1120,160]{2,3,1,0:T(8,128)(2,1)} copy(bf16[1,4,1120,160]{3,2,1,0:T(8,128)(2,1)} %bitcast.47) | data formatting | bytes 2867200 | tf_op jit(solution)/shard_map/stack | solution.py:63
  66.9 3.3 %multiply_convert_fusion.1 = bf16[4,7,160,160]{2,3,1,0:T(8,128)(2,1)} fusion(f32[7]{0:T(128)S(1)} %multiply_bitcast_fusion, bf16[7,4,48,160]{3,2,0,1:T(8,128)(2,1)} %bitcast.49, bf16[4,48,160,1]{2,1,3,0:T(8,128)(2,1)S(1)} %bitcast.59), kind=kOutput, calls=%fused_computation.2 | convolution fusion | flops 70246400 | bytes 1925148 | tf_op jit(solution)/shard_map/fka,pfkb->fpab/dot_general | solution.py:58
  70.2 4.0 %copy.28 = bf16[1,4,1120,160]{2,3,1,0:T(8,128)(2,1)} copy(bf16[1,4,1120,160]{3,2,1,0:T(8,128)(2,1)} %bitcast.46) | data formatting | bytes 2867200 | tf_op jit(solution)/shard_map/stack | solution.py:63
  74.1 3.8 %pad_maximum_fusion = bf16[2,4,1120,160]{2,3,1,0:T(8,128)(2,1)} fusion(bf16[1,4,1120,160]{2,3,1,0:T(8,128)(2,1)} %copy.29, bf16[1,4,1120,160]{2,3,1,0:T(8,128)(2,1)} %copy.28), kind=kLoop, calls=%fused_computation.3 | loop fusion | flops 1433600 | bytes 5734400 | tf_op jit(solution)/shard_map/stack | solution.py:63
  (8 shorter events, 0.1 us)
Async XLA Ops:
  0.0 1.8 %copy-start = (bf16[3,160,3000]{2,1,0:T(8,128)(2,1)S(1)}, bf16[3,160,3000]{2,1,0:T(8,128)(2,1)}, u32[]{:S(2)}) copy-start(bf16[3,160,3000]{2,1,0:T(8,128)(2,1)} %param.3) | copy-start | bytes 8640004
  0.0 8.2 %copy-start.2 = (s32[1,7]{1,0:T(1,128)S(1)}, s32[1,7]{1,0:T(1,128)}, u32[]{:S(2)}) copy-start(s32[1,7]{1,0:T(1,128)} %param.5) | copy-start | bytes 88
  0.0 8.2 %copy-start.3 = (s32[1,7]{1,0:T(1,128)S(1)}, s32[1,7]{1,0:T(1,128)}, u32[]{:S(2)}) copy-start(s32[1,7]{1,0:T(1,128)} %param.4) | copy-start | bytes 88
  3.7 10.3 %all-to-all-start = ((bf16[3,2,32,160]{3,1,0,2:T(2,128)(2,1)}), bf16[3,2,32,160]{3,1,0,2:T(2,128)(2,1)S(1)}, u32[]{:S(2)}, u32[]{:S(2)}) async-start(bf16[3,2,32,160]{3,1,0,2:T(2,128)(2,1)} %copy.21), calls=%async_computation | async-start | bytes 196608 | tf_op jit(solution)/shard_map/all_to_all | solution.py:34
  14.0 22.4 %collective-permute-start.5 = (bf16[24,2,4,160]{3,2,1,0:T(4,128)(2,1)S(1)}, bf16[24,2,4,160]{3,2,1,0:T(4,128)(2,1)S(1)}, u32[]{:S(2)}, u32[]{:S(2)}) collective-permute-start(bf16[24,2,4,160]{3,2,1,0:T(4,128)(2,1)S(1)} %bitcast.51), channel_id=1, source_target_pairs={{3,0},{4,1},{5,2},{6,3},{7,4},{8,5},{9,6},{10,7},{11,8},{12,9},{13... | collective-permute-start | bytes 184328 | tf_op jit(solution)/shard_map/ppermute | solution.py:15
  23.0 19.0 %collective-permute-start.4 = (bf16[24,2,4,160]{3,2,1,0:T(4,128)(2,1)S(1)}, bf16[24,2,4,160]{3,2,1,0:T(4,128)(2,1)}, u32[]{:S(2)}, u32[]{:S(2)}) collective-permute-start(bf16[24,2,4,160]{3,2,1,0:T(4,128)(2,1)S(1)} %bitcast.53), channel_id=1, source_target_pairs={{2,0},{3,1},{4,2},{5,3},{6,4},{7,5},{8,6},{9,7},{10,8},{11,9},{12,... | collective-permute-start | bytes 184328 | tf_op jit(solution)/shard_map/ppermute | solution.py:15
  25.5 18.3 %collective-permute-start.3 = (bf16[24,2,4,160]{3,2,1,0:T(4,128)(2,1)S(1)}, bf16[24,2,4,160]{3,2,1,0:T(4,128)(2,1)}, u32[]{:S(2)}, u32[]{:S(2)}) collective-permute-start(bf16[24,2,4,160]{3,2,1,0:T(4,128)(2,1)S(1)} %bitcast.54), channel_id=1, source_target_pairs={{1,0},{2,1},{3,2},{4,3},{5,4},{6,5},{7,6},{8,7},{9,8},{10,9},{11,1... | collective-permute-start | bytes 184328 | tf_op jit(solution)/shard_map/ppermute | solution.py:15
  27.9 17.6 %collective-permute-start.2 = (bf16[24,2,4,160]{3,2,1,0:T(4,128)(2,1)S(1)}, bf16[24,2,4,160]{3,2,1,0:T(4,128)(2,1)}, u32[]{:S(2)}, u32[]{:S(2)}) collective-permute-start(bf16[24,2,4,160]{3,2,1,0:T(4,128)(2,1)S(1)} %bitcast.55), channel_id=1, source_target_pairs={{0,1},{1,2},{2,3},{3,4},{4,5},{5,6},{6,7},{7,8},{8,9},{9,10},{10,1... | collective-permute-start | bytes 184328 | tf_op jit(solution)/shard_map/ppermute | solution.py:15
  31.4 15.8 %collective-permute-start.1 = (bf16[24,2,4,160]{3,2,1,0:T(4,128)(2,1)S(1)}, bf16[24,2,4,160]{3,2,1,0:T(4,128)(2,1)S(1)}, u32[]{:S(2)}, u32[]{:S(2)}) collective-permute-start(bf16[24,2,4,160]{3,2,1,0:T(4,128)(2,1)S(1)} %bitcast.56), channel_id=1, source_target_pairs={{0,2},{1,3},{2,4},{3,5},{4,6},{5,7},{6,8},{7,9},{8,10},{9,11},{10,... | collective-permute-start | bytes 184328 | tf_op jit(solution)/shard_map/ppermute | solution.py:15
  36.5 13.1 %collective-permute-start = (bf16[24,2,4,160]{3,2,1,0:T(4,128)(2,1)S(1)}, bf16[24,2,4,160]{3,2,1,0:T(4,128)(2,1)}, u32[]{:S(2)}, u32[]{:S(2)}) collective-permute-start(bf16[24,2,4,160]{3,2,1,0:T(4,128)(2,1)S(1)} %bitcast.58), channel_id=1, source_target_pairs={{0,3},{1,4},{2,5},{3,6},{4,7},{5,8},{6,9},{7,10},{8,11},{9,12},{10... | collective-permute-start | bytes 184328 | tf_op jit(solution)/shard_map/ppermute | solution.py:15
  58.9 0.9 %copy-start.1 = (bf16[7,4,2,24,160]{4,3,2,0,1:T(8,128)(2,1)}, bf16[7,4,2,24,160]{4,3,2,0,1:T(8,128)(2,1)S(1)}, u32[]{:S(2)}) copy-start(bf16[7,4,2,24,160]{4,3,2,0,1:T(8,128)(2,1)S(1)} %copy.25) | copy-start | bytes 1290244
where the time goes:
time: 78.9 us; the launch traced here: 77.9 us
  starting transfers between devices  30 us (38%)
  local copies, waits for them, and re-layouts  25.9 us (33%)
  matrix products  8.61 us (11%)
  waiting for transfers between devices  7.43 us (9%)
  other arithmetic  5.73 us (7%)
    ppermute x6, starting transfers between devices, shifted(): return lax.ppermute(block, axis, route)  25.5 us
    another operation x8, local copies, waits for them, and re-layouts, per_device(): stacked_near = jnp.stack(neighbours, 0).reshape(2 * REACH + 1, -1)  11.8 us
    another operation x2, local copies, waits for them, and re-layouts, per_device(): jnp.stack([real_part * weight, imag_part * weight], 0).astype(jnp.bfloat16)  7.95 us
    all_to_all x1, waiting for transfers between devices, per_device(): lax.all_to_all(white, 'tm', split_axis=2, concat_axis=0, tiled=True)  5.76 us
    all_to_all x1, starting transfers between devices, per_device(): lax.all_to_all(white, 'tm', split_axis=2, concat_axis=0, tiled=True)  4.47 us
    another operation x1, other arithmetic, per_device(): jnp.stack([real_part * weight, imag_part * weight], 0).astype(jnp.bfloat16)  3.76 us
    dot_general x1, matrix products, per_device(): jnp.einsum('fka,pfkb->fpab', own_cat, other_cat, preferred_element_type=j...  3.29 us
    dot_general x1, matrix products, per_device(): jnp.einsum('fka,pfkb->fpab', own_swap, other_cat, preferred_element_type=...  3.09 us
  transfers between devices with their start and end apart: 7, of which 2 were waited for; matrix products, arithmetic and copies ran while one was open for 11% of the time, Pallas kernels for 0%

commit v1 on v0

v1 whole, which is shorter than its diff:
```python
import functools
import math

import jax
import jax.numpy as jnp
import numpy as np
from jax import lax
from jax.experimental import pallas as pl
from jax.experimental.pallas import tpu as pltpu
from jax.sharding import Mesh
from jax.sharding import PartitionSpec as P

BINS = 32
REACH = 3
SLOTS = 7
WIDTH = 160
LANES = 128
TAIL = WIDTH - LANES
TM = 8
SEG_LOCAL = 3
LOCAL_BINS = BINS // TM
ROWS = 32
DEPTH = 64
USED = 2 * SEG_LOCAL * TM
SPAN = 4 * WIDTH


def spectra_table(length):
    times = np.arange(length, dtype=np.int64)
    freqs = 60 + 10 * np.arange(BINS, dtype=np.int64)
    phase = (freqs[:, None] * times[None, :]) % length
    angle = phase.astype(np.float32) * np.float32(2.0 * math.pi / length)
    both = np.stack([np.cos(angle), -np.sin(angle)], 0)
    both = both.reshape(2, TM, LOCAL_BINS, length).transpose(1, 0, 2, 3)
    return both.reshape(2 * BINS, length).astype(jnp.bfloat16)


def source_row(seg, part, bin_, owner):
    return owner * ROWS + (8 * SEG_LOCAL if seg is None else 8 * seg) + part * LOCAL_BINS + bin_


def depth_rows():
    rows = [(s, t, r) for s in range(SEG_LOCAL) for t in range(TM) for r in range(2)]
    return rows + [(None, t, r) for t in range(TM) for r in range(2)]


def gather_tables():
    rows = depth_rows()
    other = np.zeros((2, TM * ROWS, LOCAL_BINS * DEPTH), np.float32)
    own = np.zeros((LOCAL_BINS, 2, DEPTH, TM * ROWS), np.float32)
    for f in range(LOCAL_BINS):
        for k, (s, t, r) in enumerate(rows):
            other[0, source_row(s, r, f, t), f * DEPTH + k] = 1
            other[1, source_row(s, r, f, t), (f ^ 1) * DEPTH + k] = 1
            own[f, 0, k, source_row(s, r, f, t)] = 1
            own[f, 1, k, source_row(s, 1 - r, f, t)] = 1 if r == 0 else -1
    return other.astype(jnp.bfloat16), own.reshape(LOCAL_BINS, 2 * DEPTH, -1).astype(jnp.bfloat16)


def whiten_kernel(table_ref, records_ref, out_ref, tail_ref):
    s = pl.program_id(0)
    spectrum = lax.dot_general(
        table_ref[...],
        records_ref[0],
        (((1,), (1,)), ((), ())),
        preferred_element_type=jnp.float32,
    )
    power = jnp.mean(spectrum * spectrum, axis=0, keepdims=True)
    white = spectrum * lax.rsqrt(power + 1e-06)
    main = white[:, :LANES].astype(jnp.bfloat16).reshape(TM, 8, LANES)
    last = jnp.pad(white[:, LANES:], ((0, 0), (0, LANES - TAIL)))
    for step in range(SEG_LOCAL):

        @pl.when(s == step)
        def _():
            for copy in range(2):
                out_ref[:, copy, 8 * step : 8 * step + 8, :] = main
            if step == 0:
                tail_ref[...] = last
            else:
                tail_ref[...] += pltpu.roll(last, TAIL * step, 1)
            if step == SEG_LOCAL - 1:
                tails = tail_ref[...].astype(jnp.bfloat16).reshape(TM, 8, LANES)
                for copy in range(2):
                    out_ref[:, copy, 8 * SEG_LOCAL :, :] = tails


def whiten(records, table):
    length = records.shape[2]
    return pl.pallas_call(
        whiten_kernel,
        grid=(SEG_LOCAL,),
        in_specs=[
            pl.BlockSpec((2 * BINS, length), lambda s: (0, 0)),
            pl.BlockSpec((1, WIDTH, length), lambda s: (s, 0, 0)),
        ],
        out_specs=pl.BlockSpec((TM, 2, ROWS, LANES), lambda s: (0, 0, 0, 0)),
        out_shape=jax.ShapeDtypeStruct((TM, 2, ROWS, LANES), jnp.bfloat16),
        scratch_shapes=[pltpu.VMEM((2 * BINS, LANES), jnp.float32)],
        compiler_params=pltpu.CompilerParams(vmem_limit_bytes=32 << 20),
    )(table, records)


def stack_kernel(
    offset_ref, valid_ref, odd_ref, mine_ref, near_ref, far_ref, edge_ref, gather_ref, own_ref,
    out_ref, left_ref, block_ref,
):
    f = pl.program_id(0)
    odd = odd_ref[0]

    @pl.when(f == 0)
    def _():
        for i in range(2):
            block_ref[i] = near_ref[:, i].reshape(TM * ROWS, LANES)
            block_ref[2 + i] = mine_ref[:, i].reshape(TM * ROWS, LANES)
            block_ref[4 + i] = far_ref[:, i].reshape(TM * ROWS, LANES)
        block_ref[6] = edge_ref[...].reshape(TM * ROWS, LANES)
        lane = lax.broadcasted_iota(jnp.int32, (TAIL, 4 * DEPTH), 1) % DEPTH
        halves = [None, None]
        for p in range(8):
            if p < SLOTS:
                d = offset_ref[0, p]
                at_even = jnp.where(d == -3, 6, d + 2)
                at_odd = jnp.where(
                    d == 3, 6, jnp.where(d <= -2, d + 7, jnp.where(d <= 0, d + 3, d - 1))
                )
                block = block_ref[jnp.where(odd == 1, at_odd, at_even)]
                turned = lax.dot_general(
                    block,
                    gather_ref[p % 2],
                    (((0,), (0,)), ((), ())),
                    preferred_element_type=jnp.float32,
                )
                last = jnp.zeros((TAIL, 4 * DEPTH), jnp.float32)
                for s in range(SEG_LOCAL):
                    moved = pltpu.roll(
                        turned[TAIL * s : TAIL * (s + 1)], (16 * s - USED) % (4 * DEPTH), 1
                    )
                    last = jnp.where((lane >= 16 * s) & (lane < 16 * s + 16), moved, last)
                halves[p % 2] = jnp.concatenate([turned, last], 0)
            else:
                halves[p % 2] = jnp.zeros((WIDTH, 4 * DEPTH), jnp.float32)
            if p % 2 == 1:
                low = lax.broadcasted_iota(jnp.int32, (WIDTH, LANES), 1) < DEPTH
                for g in range(LOCAL_BINS):
                    tile = slice(LANES * (g // 2), LANES * (g // 2 + 1))
                    first, second = halves if g % 2 == 0 else halves[::-1]
                    pair = jnp.where(low, first[:, tile], second[:, tile])
                    left_ref[
                        g,
                        WIDTH * (p // 4) : WIDTH * (p // 4 + 1),
                        LANES * (p % 4 // 2) : LANES * (p % 4 // 2 + 1),
                    ] = pair.astype(jnp.bfloat16)

    own = jnp.where(odd == 1, mine_ref[:, 1], mine_ref[:, 0]).reshape(TM * ROWS, LANES)
    ordered = jnp.dot(own_ref[0], own, preferred_element_type=jnp.float32)
    lane = lax.broadcasted_iota(jnp.int32, (USED, LANES), 1)
    zero = jnp.zeros((DEPTH, LANES), jnp.bfloat16)
    fill = jnp.zeros((DEPTH - USED, LANES), jnp.bfloat16)
    column = lax.broadcasted_iota(jnp.int32, (1, 2 * SPAN), 1)
    weight = jnp.zeros((1, 2 * SPAN), jnp.float32)
    for p in range(SLOTS):
        here = (column >= WIDTH * p) & (column < WIDTH * (p + 1))
        weight = jnp.where(here, valid_ref[0, p].astype(jnp.float32), weight)
    weight = weight * (1.0 / math.sqrt(SEG_LOCAL * TM))
    for part in range(2):
        rows = ordered[DEPTH * part : DEPTH * (part + 1)]
        main, last = rows[:USED], rows[USED:]
        turns = [last if m == 0 else pltpu.roll(last, TAIL * m, 1) for m in range(4)]
        tiles = []
        for j in range(4):
            moved = main if j == 0 else pltpu.roll(main, TAIL * j, 1)
            ends = jnp.concatenate([turns[(j - s) % 4] for s in range(SEG_LOCAL)], 0)
            low = jnp.where(lane >= TAIL * j, moved, 0.0)
            high = jnp.where(
                lane < TAIL * j, moved, jnp.where(lane < TAIL * (j + 1), ends, 0.0)
            )
            tiles.append(
                [jnp.concatenate([x.astype(jnp.bfloat16), fill], 0) for x in (low, high)]
            )
        grid_rows = [
            jnp.concatenate(
                [tiles[j][c - j] if 0 <= c - j < 2 else zero for c in range(5)], 1
            )
            for j in range(4)
        ]
        swapped = [grid_rows[j] for j in (1, 0, 3, 2)]
        even = jnp.concatenate(grid_rows, 0)
        odd_f = jnp.concatenate(swapped, 0)
        right = jnp.where(f % 2 == 0, even, odd_f)
        product = jnp.dot(left_ref[f], right, preferred_element_type=jnp.float32)
        out_ref[part, 0, :, :SPAN] = (product[:WIDTH] * weight[:, :SPAN]).astype(jnp.bfloat16)
        out_ref[part, 0, :, SPAN:] = (
            product[WIDTH:, : SLOTS * WIDTH - SPAN] * weight[:, SPAN : SLOTS * WIDTH]
        ).astype(jnp.bfloat16)


def stack(offsets, valid, odd, mine, near, far, edge, gather, own):
    whole = lambda *shape: pl.BlockSpec(shape, lambda f: (0,) * len(shape))
    scalars = pl.BlockSpec(memory_space=pltpu.SMEM)
    return pl.pallas_call(
        stack_kernel,
        grid=(LOCAL_BINS,),
        in_specs=[
            scalars,
            scalars,
            scalars,
            whole(TM, 2, ROWS, LANES),
            whole(TM, 2, ROWS, LANES),
            whole(TM, 2, ROWS, LANES),
            whole(TM, ROWS, LANES),
            whole(2, TM * ROWS, LOCAL_BINS * DEPTH),
            pl.BlockSpec((1, 2 * DEPTH, TM * ROWS), lambda f: (f, 0, 0)),
        ],
        out_specs=pl.BlockSpec((2, 1, WIDTH, SLOTS * WIDTH), lambda f: (0, f, 0, 0)),
        out_shape=jax.ShapeDtypeStruct((2, LOCAL_BINS, WIDTH, SLOTS * WIDTH), jnp.bfloat16),
        scratch_shapes=[
            pltpu.VMEM((LOCAL_BINS, 2 * WIDTH, 4 * DEPTH), jnp.bfloat16),
            pltpu.VMEM((SLOTS, TM * ROWS, LANES), jnp.bfloat16),
        ],
        compiler_params=pltpu.CompilerParams(vmem_limit_bytes=32 << 20),
    )(offsets, valid, odd, mine, near, far, edge, gather, own)


def per_device(records, partner, valid):
    blocks = lax.axis_size("pair") * 2
    chan = ("pair", "side")
    side = lax.axis_index("side")
    table = jnp.asarray(spectra_table(records.shape[2]))
    gather, own = (jnp.asarray(x) for x in gather_tables())

    def fetch(array, even, odd):
        route = [((c + (odd if c % 2 else even)) % blocks, c) for c in range(blocks)]
        return lax.ppermute(array, chan, route)

    white = whiten(records, table)
    mine = lax.all_to_all(
        white.reshape(2 * TM, ROWS, LANES), ("tm", "side"), 0, 0, tiled=True
    ).reshape(TM, 2, ROWS, LANES)
    near = fetch(mine, -1, 1)
    far = fetch(mine, 2, -2)
    edge = fetch(lax.dynamic_index_in_dim(far, side, 1, keepdims=False), -1, 1)
    offsets = partner - (lax.axis_index("pair") * 2 + side)
    result = stack(offsets, valid, side.reshape(1), mine, near, far, edge, gather, own)
    return jnp.transpose(result, (0, 1, 3, 2))


def solution(mesh):
    tm, chan = mesh.shape["tm"], mesh.shape["chan"]
    paired = Mesh(mesh.devices.reshape(tm, chan // 2, 2), ("tm", "pair", "side"))
    blocks = ("pair", "side")
    return jax.shard_map(
        per_device,
        mesh=paired,
        in_specs=(P("tm", blocks, None), P(blocks, None), P(blocks, None)),
        out_specs=P(None, "tm", blocks, None),
        check_vma=False,
    )
```

time: 78.9 us -> 39.7 us (0.50)
  the two profiles are of different devices: /device:TPU:6 before, /device:TPU:8 now
where the time goes in v1:
time: 39.7 us; the launch traced here: 39.5 us
  blocking collectives  11.3 us (28%)
  starting transfers between devices  10.2 us (26%)
  waiting for transfers between devices  8.87 us (22%)
  Pallas kernels  6.27 us (16%)
  local copies, waits for them, and re-layouts  2.85 us (7%)
    all_to_all x1, blocking collectives, per_device(): lax.all_to_all(white.reshape(2 * TM, ROWS, LANES), ('tm', 'side'), 0, 0,...  11.3 us
    ppermute x3, starting transfers between devices, fetch(): return lax.ppermute(array, chan, route)  10.2 us
    ppermute x3, waiting for transfers between devices, fetch(): return lax.ppermute(array, chan, route)  8.87 us
    pallas_call x1, Pallas kernels, stack(): pl.pallas_call(stack_kernel, grid=(LOCAL_BINS,), in_specs=[scalars, scala...  4.69 us
    unnamed x12, local copies, waits for them, and re-layouts  2.84 us
    pallas_call x1, Pallas kernels, whiten(): pl.pallas_call(whiten_kernel, grid=(SEG_LOCAL,), in_specs=[pl.BlockSpec((...  1.58 us
  transfers between devices with their start and end apart: 3, of which 3 were waited for; matrix products, arithmetic and copies ran while one was open for 0% of the time, Pallas kernels for 0%

profile of v1, /device:TPU:8, one launch (start us, length us, event | category | flops | bytes accessed | tf_op | source)
XLA Modules:
  0.0 39.5 jit_solution(4772473822628035063)
XLA Ops:
  0.0 0.0 copy-start
  0.0 1.8 %copy-done = bf16[3,160,3000]{2,1,0:T(8,128)(2,1)S(1)} copy-done((bf16[3,160,3000]{2,1,0:T(8,128)(2,1)S(1)}, bf16[3,160,3000]{2,1,0:T(8,128)(2,1)}, u32[]{:S(2)}) %copy-start) | copy-done | bytes 2880024
  1.8 0.0 copy-start.1
  1.8 1.0 %copy-done.1 = bf16[64,3000]{1,0:T(8,128)(2,1)S(1)} copy-done((bf16[64,3000]{1,0:T(8,128)(2,1)S(1)}, bf16[64,3000]{1,0:T(8,128)(2,1)}, u32[]{:S(2)}) %copy-start.1) | copy-done | bytes 384024
  2.8 0.0 copy-start.5
  2.8 0.0 copy-start.2
  2.8 0.0 copy-start.3
  2.8 0.0 copy-start.4
  2.8 1.6 %shard_map.64 = bf16[8,2,32,128]{3,2,1,0:T(8,128)(2,1)S(1)} custom-call(bf16[64,3000]{1,0:T(8,128)(2,1)S(1)} %copy-done.1, bf16[3,160,3000]{2,1,0:T(8,128)(2,1)S(1)} %copy-done), custom_call_target="tpu_custom_call" | custom-call | tf_op jit(solution)/shard_map/pallas_call | solution.py:90
  4.4 11.3 %all_to_all.5 = bf16[16,32,128]{2,1,0:T(8,128)(2,1)S(1)} all-to-all(bf16[16,32,128]{2,1,0:T(8,128)(2,1)S(1)} %bitcast.9), channel_id=1, replica_groups=mesh['tm'=8,'pair'=16,'side'=2] {'tm','side'}, dimensions={0} | all-to-all | bytes 262144 | tf_op jit(solution)/shard_map/all_to_all | solution.py:237
  15.7 7.6 %collective-permute-start.1 = (bf16[8,2,32,128]{3,2,1,0:T(8,128)(2,1)S(1)}, bf16[8,2,32,128]{3,2,1,0:T(8,128)(2,1)S(1)}, u32[]{:S(2)}, u32[]{:S(2)}) collective-permute-start(bf16[8,2,32,128]{3,2,1,0:T(8,128)(2,1)S(1)} %bitcast.6), channel_id=1, source_target_pairs={{2,0},{31,1},{4,2},{1,3},{6,4},{3,5},{8,6},{5,7},{10,8},{7,9},{12,... | collective-permute-start | bytes 393224 | tf_op jit(solution)/shard_map/ppermute | solution.py:234
  23.3 0.0 collective-permute-start
  23.3 3.9 %collective-permute-done.1.far_ref = bf16[8,2,32,128]{3,2,1,0:T(8,128)(2,1)S(1)} collective-permute-done((bf16[8,2,32,128]{3,2,1,0:T(8,128)(2,1)S(1)}, bf16[8,2,32,128]{3,2,1,0:T(8,128)(2,1)S(1)}, u32[]{:S(2)}, u32[]{:S(2)}) %collective-permute-start.1) | collective-permute-done | bytes 131104 | tf_op jit(solution)/shard_map/ppermute | solution.py:234
  27.2 2.6 %collective-permute-start.2 = (bf16[8,32,128]{2,1,0:T(8,128)(2,1)S(1)}, bf16[8,32,128]{2,1,0:T(8,128)(2,1)S(1)}, u32[]{:S(2)}, u32[]{:S(2)}) collective-permute-start(bf16[8,32,128]{2,1,0:T(8,128)(2,1)S(1)} %dynamic-slice_bitcast_fusion), channel_id=1, source_target_pairs={{31,0},{2,1},{1,2},{4,3},{3,4},{6,5},{5,6},{8,7},{7,8},{10,9},{9,1... | collective-permute-start | bytes 196616 | tf_op jit(solution)/shard_map/ppermute | solution.py:234
  29.8 0.0 copy-done.5
  29.8 2.4 %collective-permute-done.near_ref = bf16[8,2,32,128]{3,2,1,0:T(8,128)(2,1)S(1)} collective-permute-done((bf16[8,2,32,128]{3,2,1,0:T(8,128)(2,1)S(1)}, bf16[8,2,32,128]{3,2,1,0:T(8,128)(2,1)S(1)}, u32[]{:S(2)}, u32[]{:S(2)}) %collective-permute-start) | collective-permute-done | bytes 131104 | tf_op jit(solution)/shard_map/ppermute | solution.py:234
  32.2 2.6 %collective-permute-done.2.edge_ref = bf16[8,32,128]{2,1,0:T(8,128)(2,1)S(1)} collective-permute-done((bf16[8,32,128]{2,1,0:T(8,128)(2,1)S(1)}, bf16[8,32,128]{2,1,0:T(8,128)(2,1)S(1)}, u32[]{:S(2)}, u32[]{:S(2)}) %collective-permute-start.2) | collective-permute-done | bytes 65568 | tf_op jit(solution)/shard_map/ppermute | solution.py:234
  34.8 0.0 copy-done.2
  34.8 0.0 copy-done.3
  34.8 0.0 copy-done.4
  34.8 4.7 %shard_map.65 = bf16[2,4,160,1120]{3,2,1,0:T(8,128)(2,1)} custom-call(s32[1,7]{1,0:T(1,128)S(1)} %broadcast_subtract_fusion.offset_ref, s32[1,7]{1,0:T(1,128)S(1)} %copy-done.4, s32[1]{0:T(128)} %bitcast.odd_ref, bf16[8,2,32,128]{3,2,1,0:T(8,128)(2,1)S(1)} %bitcast.8, bf16[8,2,32,128]{3,2,1,0:T(8,128)(2,1)S(1)} %collective-permute-done.near_ref, ...), custom_call_target="tpu_custom_call" | custom-call | tf_op jit(solution)/shard_map/pallas_call | solution.py:201
  (2 shorter events, 0.0 us)
Async XLA Ops:
  0.0 1.8 %copy-start = (bf16[3,160,3000]{2,1,0:T(8,128)(2,1)S(1)}, bf16[3,160,3000]{2,1,0:T(8,128)(2,1)}, u32[]{:S(2)}) copy-start(bf16[3,160,3000]{2,1,0:T(8,128)(2,1)} %records_ref.1) | copy-start | bytes 8640004
  1.8 1.0 %copy-start.1 = (bf16[64,3000]{1,0:T(8,128)(2,1)S(1)}, bf16[64,3000]{1,0:T(8,128)(2,1)}, u32[]{:S(2)}) copy-start(bf16[64,3000]{1,0:T(8,128)(2,1)} %constant.21.clone.table_ref) | copy-start | bytes 1152004
  2.8 26.9 %copy-start.5 = (s32[1,7]{1,0:T(1,128)S(1)}, s32[1,7]{1,0:T(1,128)}, u32[]{:S(2)}) copy-start(s32[1,7]{1,0:T(1,128)} %param.7) | copy-start | bytes 88
  2.8 32.0 %copy-start.2 = (bf16[4,128,256]{2,1,0:T(8,128)(2,1)S(1)}, bf16[4,128,256]{2,1,0:T(8,128)(2,1)}, u32[]{:S(2)}) copy-start(bf16[4,128,256]{2,1,0:T(8,128)(2,1)} %constant.23.clone.own_ref) | copy-start | bytes 786436
  2.8 32.0 %copy-start.3 = (bf16[2,256,256]{2,1,0:T(8,128)(2,1)S(1)}, bf16[2,256,256]{2,1,0:T(8,128)(2,1)}, u32[]{:S(2)}) copy-start(bf16[2,256,256]{2,1,0:T(8,128)(2,1)} %constant.22.clone.gather_ref) | copy-start | bytes 786436
  2.8 32.0 %copy-start.4 = (s32[1,7]{1,0:T(1,128)S(1)}, s32[1,7]{1,0:T(1,128)}, u32[]{:S(2)}) copy-start(s32[1,7]{1,0:T(1,128)} %valid_ref.1) | copy-start | bytes 88
  15.7 11.5 %collective-permute-start.1 = (bf16[8,2,32,128]{3,2,1,0:T(8,128)(2,1)S(1)}, bf16[8,2,32,128]{3,2,1,0:T(8,128)(2,1)S(1)}, u32[]{:S(2)}, u32[]{:S(2)}) collective-permute-start(bf16[8,2,32,128]{3,2,1,0:T(8,128)(2,1)S(1)} %bitcast.6), channel_id=1, source_target_pairs={{2,0},{31,1},{4,2},{1,3},{6,4},{3,5},{8,6},{5,7},{10,8},{7,9},{12,... | collective-permute-start | bytes 393224 | tf_op jit(solution)/shard_map/ppermute | solution.py:234
  23.3 8.8 %collective-permute-start = (bf16[8,2,32,128]{3,2,1,0:T(8,128)(2,1)S(1)}, bf16[8,2,32,128]{3,2,1,0:T(8,128)(2,1)S(1)}, u32[]{:S(2)}, u32[]{:S(2)}) collective-permute-start(bf16[8,2,32,128]{3,2,1,0:T(8,128)(2,1)S(1)} %bitcast.7), channel_id=1, source_target_pairs={{31,0},{2,1},{1,2},{4,3},{3,4},{6,5},{5,6},{8,7},{7,8},{10,9},{9,1... | collective-permute-start | bytes 393224 | tf_op jit(solution)/shard_map/ppermute | solution.py:234
  27.2 7.6 %collective-permute-start.2 = (bf16[8,32,128]{2,1,0:T(8,128)(2,1)S(1)}, bf16[8,32,128]{2,1,0:T(8,128)(2,1)S(1)}, u32[]{:S(2)}, u32[]{:S(2)}) collective-permute-start(bf16[8,32,128]{2,1,0:T(8,128)(2,1)S(1)} %dynamic-slice_bitcast_fusion), channel_id=1, source_target_pairs={{31,0},{2,1},{1,2},{4,3},{3,4},{6,5},{5,6},{8,7},{7,8},{10,9},{9,1... | collective-permute-start | bytes 196616 | tf_op jit(solution)/shard_map/ppermute | solution.py:234

commit v2 on v0

v2 whole, which is shorter than its diff:
```python
import functools
import math

import jax
import jax.numpy as jnp
import numpy as np
from jax import lax
from jax.experimental import pallas as pl
from jax.experimental.pallas import tpu as pltpu
from jax.sharding import Mesh
from jax.sharding import PartitionSpec as P

BINS = 32
REACH = 3
SLOTS = 7
WIDTH = 160
LANES = 128
TAIL = WIDTH - LANES
TM = 8
SEG_LOCAL = 3
LOCAL_BINS = BINS // TM
ROWS = 32
DEPTH = 64
USED = 2 * SEG_LOCAL * TM
SPAN = 4 * WIDTH
CHUNK = 512
SCOPE = 32 << 20
SPARE = 7
WHOLE = 56_000_000


def spectra_table(length):
    times = np.arange(length, dtype=np.int64)
    freqs = 60 + 10 * np.arange(BINS, dtype=np.int64)
    phase = (freqs[:, None] * times[None, :]) % length
    angle = phase.astype(np.float32) * np.float32(2.0 * math.pi / length)
    both = np.stack([np.cos(angle), -np.sin(angle)], 0)
    both = both.reshape(2, TM, LOCAL_BINS, length).transpose(1, 0, 2, 3)
    table = both.reshape(1, 2 * BINS, length).astype(jnp.bfloat16)
    return np.concatenate([table, np.zeros((SPARE, 2 * BINS, length), table.dtype)], 0)


def source_row(seg, part, bin_, owner):
    return owner * ROWS + (8 * SEG_LOCAL if seg is None else 8 * seg) + part * LOCAL_BINS + bin_


def depth_rows():
    rows = [(s, t, r) for s in range(SEG_LOCAL) for t in range(TM) for r in range(2)]
    return rows + [(None, t, r) for t in range(TM) for r in range(2)]


def gather_tables():
    rows = depth_rows()
    other = np.zeros((2, TM * ROWS, LOCAL_BINS * LANES), np.float32)
    own = np.zeros((LOCAL_BINS, 2, DEPTH, TM * ROWS), np.float32)
    for f in range(LOCAL_BINS):
        for k, (s, t, r) in enumerate(rows):
            for order in range(2):
                other[order, source_row(s, r, f, t), f * LANES + order * DEPTH + k] = 1
            own[f, 0, k, source_row(s, r, f, t)] = 1
            own[f, 1, k, source_row(s, 1 - r, f, t)] = 1 if r == 0 else -1
    return other.astype(jnp.bfloat16), own.reshape(LOCAL_BINS, 2 * DEPTH, -1).astype(jnp.bfloat16)


def whiten_kernel(table_hbm, records_hbm, out_ref, table_ref, records_ref, sems):
    length = records_ref.shape[2]
    edges = list(range(0, length, CHUNK)) + [length]
    cuts = [slice(a, b) for a, b in zip(edges[:-1], edges[1:])]
    copies = []
    for i, cut in enumerate(cuts):
        part = pl.ds(cut.start, cut.stop - cut.start)
        if i == 0:
            copies.append(pltpu.make_async_copy(table_hbm.at[0], table_ref, sems.at[len(cuts)]))
        copies.append(
            pltpu.make_async_copy(
                records_hbm.at[:, :, part], records_ref.at[:, :, part], sems.at[i]
            )
        )
    for copy in copies:
        copy.start()
    copies[0].wait()
    total = None
    for i, cut in enumerate(cuts):
        copies[i + 1].wait()
        product = lax.dot_general(
            table_ref[:, cut],
            records_ref[:, :, cut].reshape(SEG_LOCAL * WIDTH, cut.stop - cut.start),
            (((1,), (1,)), ((), ())),
            preferred_element_type=jnp.float32,
        )
        total = product if total is None else total + product
    tails = None
    for s in range(SEG_LOCAL):
        spectrum = total[:, WIDTH * s : WIDTH * (s + 1)]
        power = jnp.mean(spectrum * spectrum, axis=0, keepdims=True)
        white = spectrum * lax.rsqrt(power + 1e-06)
        main = white[:, :LANES].astype(jnp.bfloat16).reshape(TM, 8, LANES)
        last = jnp.pad(white[:, LANES:], ((0, 0), (0, LANES - TAIL)))
        tails = last if s == 0 else tails + pltpu.roll(last, TAIL * s, 1)
        for copy in range(2):
            out_ref[:, copy, 8 * s : 8 * s + 8, :] = main
    tails = tails.astype(jnp.bfloat16).reshape(TM, 8, LANES)
    for copy in range(2):
        out_ref[:, copy, 8 * SEG_LOCAL :, :] = tails


def whiten(records, table):
    cuts = -(-records.shape[2] // CHUNK)
    return pl.pallas_call(
        whiten_kernel,
        in_specs=[pl.BlockSpec(memory_space=pltpu.HBM)] * 2,
        out_specs=pl.BlockSpec(memory_space=pltpu.VMEM),
        out_shape=jax.ShapeDtypeStruct((TM, 2, ROWS, LANES), jnp.bfloat16),
        scratch_shapes=[
            pltpu.VMEM(table.shape[1:], jnp.bfloat16),
            pltpu.VMEM(records.shape, jnp.bfloat16),
            pltpu.SemaphoreType.DMA((cuts + 1,)),
        ],
        compiler_params=pltpu.CompilerParams(vmem_limit_bytes=WHOLE),
    )(table, records)


def spread_kernel(odd_ref, mine_ref, own_ref, out_ref):
    own = jnp.where(odd_ref[0] == 1, mine_ref[:, 1], mine_ref[:, 0]).reshape(TM * ROWS, LANES)
    lane = lax.broadcasted_iota(jnp.int32, (USED, LANES), 1)
    fill = jnp.zeros((DEPTH - USED, LANES), jnp.bfloat16)
    for f in range(LOCAL_BINS):
        ordered = jnp.dot(own_ref[f], own, preferred_element_type=jnp.float32)
        for part in range(2):
            rows = ordered[DEPTH * part : DEPTH * (part + 1)]
            main, last = rows[:USED], rows[USED:]
            turns = [last if m == 0 else pltpu.roll(last, TAIL * m, 1) for m in range(4)]
            for j in range(4):
                moved = main if j == 0 else pltpu.roll(main, TAIL * j, 1)
                ends = jnp.concatenate([turns[(j - s) % 4] for s in range(SEG_LOCAL)], 0)
                low = jnp.where(lane >= TAIL * j, moved, 0.0)
                high = jnp.where(
                    lane < TAIL * j, moved, jnp.where(lane < TAIL * (j + 1), ends, 0.0)
                )
                for half, x in enumerate((low, high)):
                    tile = slice(LANES * half, LANES * (half + 1))
                    out_ref[f, part, j, :USED, tile] = x.astype(jnp.bfloat16)
                    out_ref[f, part, j, USED:, tile] = fill


def spread(odd, mine, own):
    shape = (LOCAL_BINS, 2, 4, DEPTH, 2 * LANES)
    return pl.pallas_call(
        spread_kernel,
        in_specs=[pl.BlockSpec(memory_space=pltpu.SMEM)]
        + [pl.BlockSpec(memory_space=pltpu.VMEM)] * 2,
        out_specs=pl.BlockSpec(memory_space=pltpu.VMEM),
        out_shape=jax.ShapeDtypeStruct(shape, jnp.bfloat16),
        compiler_params=pltpu.CompilerParams(vmem_limit_bytes=SCOPE),
        cost_estimate=pl.CostEstimate(flops=70_000_000, bytes_accessed=3_000_000, transcendentals=0),
    )(odd, mine, own)


def turned(block, gather):
    lane = lax.broadcasted_iota(jnp.int32, (TAIL, LOCAL_BINS * LANES), 1) % DEPTH
    whole = lax.dot_general(
        block, gather, (((0,), (0,)), ((), ())), preferred_element_type=jnp.float32
    )
    last = jnp.zeros((TAIL, LOCAL_BINS * LANES), jnp.float32)
    for s in range(SEG_LOCAL):
        moved = whole[TAIL * s : TAIL * (s + 1)]
        moved = pltpu.roll(moved, (16 * s - USED) % (LOCAL_BINS * LANES), 1)
        last = jnp.where((lane >= 16 * s) & (lane < 16 * s + 16), moved, last)
    return jnp.concatenate([whole, last], 0).astype(jnp.bfloat16)


def turn_kernel(near_ref, mine_ref, far_ref, gather_ref, out_ref):
    for n, ref in enumerate((near_ref, mine_ref, far_ref)):
        for i in range(2):
            block = ref[:, i].reshape(TM * ROWS, LANES)
            for order in range(2):
                out_ref[2 * n + i, order] = turned(block, gather_ref[order])


def turn(near, mine, far, gather):
    shape = (SLOTS - 1, 2, WIDTH, LOCAL_BINS * LANES)
    return pl.pallas_call(
        turn_kernel,
        in_specs=[pl.BlockSpec(memory_space=pltpu.VMEM)] * 4,
        out_specs=pl.BlockSpec(memory_space=pltpu.VMEM),
        out_shape=jax.ShapeDtypeStruct(shape, jnp.bfloat16),
        compiler_params=pltpu.CompilerParams(vmem_limit_bytes=SCOPE),
        cost_estimate=pl.CostEstimate(flops=300_000_000, bytes_accessed=3_000_000, transcendentals=0),
    )(near, mine, far, gather)


def stack_kernel(
    offset_ref, valid_ref, odd_ref, ready_ref, edge_ref, gather_ref, right_ref, out_hbm,
    last_ref, out_ref, sems,
):
    odd = odd_ref[0]
    block = edge_ref[...].reshape(TM * ROWS, LANES)
    for order in range(2):
        last_ref[order] = turned(block, gather_ref[order])
    places = []
    for p in range(SLOTS):
        d = offset_ref[0, p]
        at_even = jnp.where(d == -3, 6, d + 2)
        at_odd = jnp.where(
            d == 3, 6, jnp.where(d <= -2, d + 7, jnp.where(d <= 0, d + 3, d - 1))
        )
        places.append(jnp.where(odd == 1, at_odd, at_even))
    column = lax.broadcasted_iota(jnp.int32, (1, 2 * SPAN), 1)
    weight = jnp.zeros((1, 2 * SPAN), jnp.float32)
    for p in range(SLOTS):
        here = (column >= WIDTH * p) & (column < WIDTH * (p + 1))
        weight = jnp.where(here, valid_ref[0, p].astype(jnp.float32), weight)
    weight = weight * (1.0 / math.sqrt(SEG_LOCAL * TM))
    zero = jnp.zeros((DEPTH, LANES), jnp.bfloat16)
    copies = []
    for f in range(LOCAL_BINS):
        tile = slice(LANES * f, LANES * (f + 1))

        def picked(p):
            held = ready_ref[jnp.minimum(places[p], SLOTS - 2), p % 2, :, tile]
            return jnp.where(places[p] == SLOTS - 1, last_ref[p % 2, :, tile], held)

        tiles = [
            picked(p) + picked(p + 1) if p + 1 < SLOTS else picked(p) for p in range(0, SLOTS, 2)
        ]
        left = jnp.concatenate(
            [jnp.concatenate(tiles[:2], 1), jnp.concatenate(tiles[2:], 1)], 0
        )
        for part in range(2):
            rows = []
            for j in range(4):
                here = [right_ref[f, part, j, :, :LANES], right_ref[f, part, j, :, LANES:]]
                rows.append(jnp.concatenate([zero] * j + here + [zero] * (3 - j), 1))
            product = jnp.dot(
                left, jnp.concatenate(rows, 0), preferred_element_type=jnp.float32
            )
            out_ref[part, f, :, :SPAN] = (product[:WIDTH] * weight[:, :SPAN]).astype(jnp.bfloat16)
            out_ref[part, f, :, SPAN:] = (
                product[WIDTH:, : SLOTS * WIDTH - SPAN] * weight[:, SPAN : SLOTS * WIDTH]
            ).astype(jnp.bfloat16)
            copy = pltpu.make_async_copy(
                out_ref.at[part, f], out_hbm.at[part, f], sems.at[part, f]
            )
            copy.start()
            copies.append(copy)
    for copy in copies:
        copy.wait()


def stack(offsets, valid, odd, ready, edge, gather, right):
    whole = pl.BlockSpec(memory_space=pltpu.VMEM)
    scalars = pl.BlockSpec(memory_space=pltpu.SMEM)
    shape = (2, LOCAL_BINS, WIDTH, SLOTS * WIDTH)
    return pl.pallas_call(
        stack_kernel,
        in_specs=[scalars] * 3 + [whole] * 4,
        out_specs=pl.BlockSpec(memory_space=pltpu.HBM),
        out_shape=jax.ShapeDtypeStruct(shape, jnp.bfloat16),
        scratch_shapes=[
            pltpu.VMEM((2, WIDTH, LOCAL_BINS * LANES), jnp.bfloat16),
            pltpu.VMEM(shape, jnp.bfloat16),
            pltpu.SemaphoreType.DMA((2, LOCAL_BINS)),
        ],
        compiler_params=pltpu.CompilerParams(vmem_limit_bytes=SCOPE),
    )(offsets, valid, odd, ready, edge, gather, right)


def per_device(records, partner, valid):
    blocks = lax.axis_size("pair") * 2
    chan = ("pair", "side")
    side = lax.axis_index("side")
    table = jnp.asarray(spectra_table(records.shape[2]))
    gather, own = (jnp.asarray(x) for x in gather_tables())

    def fetch(array, even, odd):
        route = [((c + (odd if c % 2 else even)) % blocks, c) for c in range(blocks)]
        return lax.ppermute(array, chan, route)

    white = whiten(records, table)
    mine = lax.all_to_all(
        white.reshape(2 * TM, ROWS, LANES), ("tm", "side"), 0, 0, tiled=True
    ).reshape(TM, 2, ROWS, LANES)
    near = fetch(mine, -1, 1)
    far = fetch(mine, 2, -2)
    edge = fetch(lax.dynamic_index_in_dim(far, side, 1, keepdims=False), -1, 1)
    offsets = partner - (lax.axis_index("pair") * 2 + side)
    odd = side.reshape(1)
    right = spread(odd, mine, own)
    ready = turn(near, mine, far, gather)
    result = stack(offsets, valid, odd, ready, edge, gather, right)
    return jnp.transpose(result, (0, 1, 3, 2))


def solution(mesh):
    tm, chan = mesh.shape["tm"], mesh.shape["chan"]
    paired = Mesh(mesh.devices.reshape(tm, chan // 2, 2), ("tm", "pair", "side"))
    blocks = ("pair", "side")
    return jax.shard_map(
        per_device,
        mesh=paired,
        in_specs=(P("tm", blocks, None), P(blocks, None), P(blocks, None)),
        out_specs=P(None, "tm", blocks, None),
        check_vma=False,
    )
```

time: 78.9 us -> 36.1 us (0.46)
  the two profiles are of different devices: /device:TPU:6 before, /device:TPU:8 now
where the time goes in v2:
time: 36.1 us; the launch traced here: 36 us
  blocking collectives  11.3 us (31%)
  starting transfers between devices  10.2 us (28%)
  waiting for transfers between devices  7.79 us (22%)
  Pallas kernels  6.62 us (18%)
    all_to_all x1, blocking collectives, per_device(): lax.all_to_all(white.reshape(2 * TM, ROWS, LANES), ('tm', 'side'), 0, 0,...  11.3 us
    ppermute x3, starting transfers between devices, fetch(): return lax.ppermute(array, chan, route)  10.2 us
    ppermute x3, waiting for transfers between devices, fetch(): return lax.ppermute(array, chan, route)  7.79 us
    pallas_call x1, Pallas kernels, stack(): pl.pallas_call(stack_kernel, in_specs=[scalars] * 3 + [whole] * 4, out_sp...  2.85 us
    pallas_call x1, Pallas kernels, whiten(): pl.pallas_call(whiten_kernel, in_specs=[pl.BlockSpec(memory_space=pltpu.H...  2.72 us
  transfers between devices with their start and end apart: 3, of which 3 were waited for; matrix products, arithmetic and copies ran while one was open for 0% of the time, Pallas kernels for 3%

profile of v2, /device:TPU:8, one launch (start us, length us, event | category | flops | bytes accessed | tf_op | source)
XLA Modules:
  0.0 36.0 jit_solution(17737226930615483860)
XLA Ops:
  0.0 0.0 copy-start.1
  0.0 0.0 copy-start
  0.0 0.0 copy-start.3
  0.0 2.7 %shard_map.64 = bf16[8,2,32,128]{3,2,1,0:T(8,128)(2,1)S(1)} custom-call(bf16[8,64,3000]{2,1,0:T(8,128)(2,1)} %constant.21.clone.table_hbm, bf16[3,160,3000]{2,1,0:T(8,128)(2,1)} %records_hbm.1), custom_call_target="tpu_custom_call" | custom-call | tf_op jit(solution)/shard_map/pallas_call | solution.py:109
  2.7 0.0 copy-start.2
  2.7 11.3 %all_to_all.5 = bf16[16,32,128]{2,1,0:T(8,128)(2,1)S(1)} all-to-all(bf16[16,32,128]{2,1,0:T(8,128)(2,1)S(1)} %bitcast.10), channel_id=1, replica_groups=mesh['tm'=8,'pair'=16,'side'=2] {'tm','side'}, dimensions={0} | all-to-all | bytes 262144 | tf_op jit(solution)/shard_map/all_to_all | solution.py:280
  14.1 7.6 %collective-permute-start.1 = (bf16[8,2,32,128]{3,2,1,0:T(8,128)(2,1)S(1)}, bf16[8,2,32,128]{3,2,1,0:T(8,128)(2,1)S(1)}, u32[]{:S(2)}, u32[]{:S(2)}) collective-permute-start(bf16[8,2,32,128]{3,2,1,0:T(8,128)(2,1)S(1)} %bitcast.6), channel_id=1, source_target_pairs={{2,0},{31,1},{4,2},{1,3},{6,4},{3,5},{8,6},{5,7},{10,8},{7,9},{12,... | collective-permute-start | bytes 393224 | tf_op jit(solution)/shard_map/ppermute | solution.py:277
  21.7 0.0 collective-permute-start
  21.7 3.9 %collective-permute-done.1.far_ref = bf16[8,2,32,128]{3,2,1,0:T(8,128)(2,1)S(1)} collective-permute-done((bf16[8,2,32,128]{3,2,1,0:T(8,128)(2,1)S(1)}, bf16[8,2,32,128]{3,2,1,0:T(8,128)(2,1)S(1)}, u32[]{:S(2)}, u32[]{:S(2)}) %collective-permute-start.1) | collective-permute-done | bytes 131104 | tf_op jit(solution)/shard_map/ppermute | solution.py:277
  25.5 2.6 %collective-permute-start.2 = (bf16[8,32,128]{2,1,0:T(8,128)(2,1)S(1)}, bf16[8,32,128]{2,1,0:T(8,128)(2,1)S(1)}, u32[]{:S(2)}, u32[]{:S(2)}) collective-permute-start(bf16[8,32,128]{2,1,0:T(8,128)(2,1)S(1)} %dynamic-slice_bitcast_fusion), channel_id=1, source_target_pairs={{31,0},{2,1},{1,2},{4,3},{3,4},{6,5},{5,6},{8,7},{7,8},{10,9},{9,1... | collective-permute-start | bytes 196616 | tf_op jit(solution)/shard_map/ppermute | solution.py:277
  28.1 0.0 copy-done.3
  28.1 0.0 copy-done.1
  28.1 0.3 shard_map.66.right_ref
  28.5 2.0 %collective-permute-done.near_ref = bf16[8,2,32,128]{3,2,1,0:T(8,128)(2,1)S(1)} collective-permute-done((bf16[8,2,32,128]{3,2,1,0:T(8,128)(2,1)S(1)}, bf16[8,2,32,128]{3,2,1,0:T(8,128)(2,1)S(1)}, u32[]{:S(2)}, u32[]{:S(2)}) %collective-permute-start) | collective-permute-done | bytes 131104 | tf_op jit(solution)/shard_map/ppermute | solution.py:277
  30.5 0.0 copy-done
  30.5 0.7 %shard_map.65.ready_ref = bf16[6,2,160,512]{3,2,1,0:T(8,128)(2,1)S(1)} custom-call(bf16[8,2,32,128]{3,2,1,0:T(8,128)(2,1)S(1)} %collective-permute-done.near_ref, bf16[8,2,32,128]{3,2,1,0:T(8,128)(2,1)S(1)} %bitcast.9, bf16[8,2,32,128]{3,2,1,0:T(8,128)(2,1)S(1)} %collective-permute-done.1.far_ref, bf16[2,256,512]{2,1,0:T(8,128)(2,1)S(1)} %copy-done), custom_call_target="tpu_custom_call" | custom-call | flops 300000000 | bytes 3000000 | tf_op jit(solution)/shard_map/pallas_call | solution.py:182
  31.2 1.9 %collective-permute-done.2.edge_ref = bf16[8,32,128]{2,1,0:T(8,128)(2,1)S(1)} collective-permute-done((bf16[8,32,128]{2,1,0:T(8,128)(2,1)S(1)}, bf16[8,32,128]{2,1,0:T(8,128)(2,1)S(1)}, u32[]{:S(2)}, u32[]{:S(2)}) %collective-permute-start.2) | collective-permute-done | bytes 65568 | tf_op jit(solution)/shard_map/ppermute | solution.py:277
  33.1 0.0 copy-done.2
  33.1 2.8 %shard_map.67 = bf16[2,4,160,1120]{3,2,1,0:T(8,128)(2,1)} custom-call(s32[1,7]{1,0:T(1,128)S(1)} %broadcast_subtract_fusion.offset_ref, s32[1,7]{1,0:T(1,128)S(1)} %copy-done.2, s32[1]{0:T(128)} %bitcast.odd_ref, bf16[6,2,160,512]{3,2,1,0:T(8,128)(2,1)S(1)} %shard_map.65.ready_ref, bf16[8,32,128]{2,1,0:T(8,128)(2,1)S(1)} %collective-permute-done.2.edge_ref, ...), custom_call_target="tpu_custom_call" | custom-call | tf_op jit(solution)/shard_map/pallas_call | solution.py:254
  (2 shorter events, 0.0 us)
Async XLA Ops:
  0.0 28.1 %copy-start.1 = (bf16[4,128,256]{2,1,0:T(8,128)(2,1)S(1)}, bf16[4,128,256]{2,1,0:T(8,128)(2,1)}, u32[]{:S(2)}) copy-start(bf16[4,128,256]{2,1,0:T(8,128)(2,1)} %constant.23.clone.own_ref) | copy-start | bytes 786436
  0.0 30.5 %copy-start = (bf16[2,256,512]{2,1,0:T(8,128)(2,1)S(1)}, bf16[2,256,512]{2,1,0:T(8,128)(2,1)}, u32[]{:S(2)}) copy-start(bf16[2,256,512]{2,1,0:T(8,128)(2,1)} %constant.22.clone.gather_ref) | copy-start | bytes 1572868
  0.0 28.1 %copy-start.3 = (s32[1,7]{1,0:T(1,128)S(1)}, s32[1,7]{1,0:T(1,128)}, u32[]{:S(2)}) copy-start(s32[1,7]{1,0:T(1,128)} %param.7) | copy-start | bytes 88
  2.7 30.4 %copy-start.2 = (s32[1,7]{1,0:T(1,128)S(1)}, s32[1,7]{1,0:T(1,128)}, u32[]{:S(2)}) copy-start(s32[1,7]{1,0:T(1,128)} %valid_ref.1) | copy-start | bytes 88
  14.1 11.5 %collective-permute-start.1 = (bf16[8,2,32,128]{3,2,1,0:T(8,128)(2,1)S(1)}, bf16[8,2,32,128]{3,2,1,0:T(8,128)(2,1)S(1)}, u32[]{:S(2)}, u32[]{:S(2)}) collective-permute-start(bf16[8,2,32,128]{3,2,1,0:T(8,128)(2,1)S(1)} %bitcast.6), channel_id=1, source_target_pairs={{2,0},{31,1},{4,2},{1,3},{6,4},{3,5},{8,6},{5,7},{10,8},{7,9},{12,... | collective-permute-start | bytes 393224 | tf_op jit(solution)/shard_map/ppermute | solution.py:277
  21.7 8.8 %collective-permute-start = (bf16[8,2,32,128]{3,2,1,0:T(8,128)(2,1)S(1)}, bf16[8,2,32,128]{3,2,1,0:T(8,128)(2,1)S(1)}, u32[]{:S(2)}, u32[]{:S(2)}) collective-permute-start(bf16[8,2,32,128]{3,2,1,0:T(8,128)(2,1)S(1)} %bitcast.7), channel_id=1, source_target_pairs={{31,0},{2,1},{1,2},{4,3},{3,4},{6,5},{5,6},{8,7},{7,8},{10,9},{9,1... | collective-permute-start | bytes 393224 | tf_op jit(solution)/shard_map/ppermute | solution.py:277
  25.5 7.6 %collective-permute-start.2 = (bf16[8,32,128]{2,1,0:T(8,128)(2,1)S(1)}, bf16[8,32,128]{2,1,0:T(8,128)(2,1)S(1)}, u32[]{:S(2)}, u32[]{:S(2)}) collective-permute-start(bf16[8,32,128]{2,1,0:T(8,128)(2,1)S(1)} %dynamic-slice_bitcast_fusion), channel_id=1, source_target_pairs={{31,0},{2,1},{1,2},{4,3},{3,4},{6,5},{5,6},{8,7},{7,8},{10,9},{9,1... | collective-permute-start | bytes 196616 | tf_op jit(solution)/shard_map/ppermute | solution.py:277

commit v3 on v2

--- a/solution.py
+++ b/solution.py
@@ -26,7 +26,7 @@
 CHUNK = 512
 SCOPE = 32 << 20
 SPARE = 7
-WHOLE = 56_000_000
+WHOLE = 54_800_000
 
 
 def spectra_table(length):
@@ -169,34 +169,34 @@
     return jnp.concatenate([whole, last], 0).astype(jnp.bfloat16)
 
 
-def turn_kernel(near_ref, mine_ref, far_ref, gather_ref, out_ref):
-    for n, ref in enumerate((near_ref, mine_ref, far_ref)):
+def turn_kernel(near_ref, mine_ref, gather_ref, out_ref):
+    for n, ref in enumerate((near_ref, mine_ref)):
         for i in range(2):
             block = ref[:, i].reshape(TM * ROWS, LANES)
             for order in range(2):
                 out_ref[2 * n + i, order] = turned(block, gather_ref[order])
 
 
-def turn(near, mine, far, gather):
-    shape = (SLOTS - 1, 2, WIDTH, LOCAL_BINS * LANES)
+def turn(near, mine, gather):
+    shape = (4, 2, WIDTH, LOCAL_BINS * LANES)
     return pl.pallas_call(
         turn_kernel,
-        in_specs=[pl.BlockSpec(memory_space=pltpu.VMEM)] * 4,
+        in_specs=[pl.BlockSpec(memory_space=pltpu.VMEM)] * 3,
         out_specs=pl.BlockSpec(memory_space=pltpu.VMEM),
         out_shape=jax.ShapeDtypeStruct(shape, jnp.bfloat16),
         compiler_params=pltpu.CompilerParams(vmem_limit_bytes=SCOPE),
-        cost_estimate=pl.CostEstimate(flops=300_000_000, bytes_accessed=3_000_000, transcendentals=0),
-    )(near, mine, far, gather)
+        cost_estimate=pl.CostEstimate(flops=200_000_000, bytes_accessed=3_000_000, transcendentals=0),
+    )(near, mine, gather)
 
 
 def stack_kernel(
-    offset_ref, valid_ref, odd_ref, ready_ref, edge_ref, gather_ref, right_ref, out_hbm,
+    offset_ref, valid_ref, odd_ref, ready_ref, far_ref, edge_ref, gather_ref, right_ref, out_hbm,
     last_ref, out_ref, sems,
 ):
     odd = odd_ref[0]
-    block = edge_ref[...].reshape(TM * ROWS, LANES)
-    for order in range(2):
-        last_ref[order] = turned(block, gather_ref[order])
+    for n, block in enumerate((far_ref[:, 0], far_ref[:, 1], edge_ref[...])):
+        for order in range(2):
+            last_ref[n, order] = turned(block.reshape(TM * ROWS, LANES), gather_ref[order])
     places = []
     for p in range(SLOTS):
         d = offset_ref[0, p]
@@ -217,8 +217,9 @@
         tile = slice(LANES * f, LANES * (f + 1))
 
         def picked(p):
-            held = ready_ref[jnp.minimum(places[p], SLOTS - 2), p % 2, :, tile]
-            return jnp.where(places[p] == SLOTS - 1, last_ref[p % 2, :, tile], held)
+            held = ready_ref[jnp.minimum(places[p], 3), p % 2, :, tile]
+            late = last_ref[jnp.maximum(places[p] - 4, 0), p % 2, :, tile]
+            return jnp.where(places[p] >= 4, late, held)
 
         tiles = [
             picked(p) + picked(p + 1) if p + 1 < SLOTS else picked(p) for p in range(0, SLOTS, 2)
@@ -247,22 +248,22 @@
         copy.wait()
 
 
-def stack(offsets, valid, odd, ready, edge, gather, right):
+def stack(offsets, valid, odd, ready, far, edge, gather, right):
     whole = pl.BlockSpec(memory_space=pltpu.VMEM)
     scalars = pl.BlockSpec(memory_space=pltpu.SMEM)
     shape = (2, LOCAL_BINS, WIDTH, SLOTS * WIDTH)
     return pl.pallas_call(
         stack_kernel,
-        in_specs=[scalars] * 3 + [whole] * 4,
+        in_specs=[scalars] * 3 + [whole] * 5,
         out_specs=pl.BlockSpec(memory_space=pltpu.HBM),
         out_shape=jax.ShapeDtypeStruct(shape, jnp.bfloat16),
         scratch_shapes=[
-            pltpu.VMEM((2, WIDTH, LOCAL_BINS * LANES), jnp.bfloat16),
+            pltpu.VMEM((3, 2, WIDTH, LOCAL_BINS * LANES), jnp.bfloat16),
             pltpu.VMEM(shape, jnp.bfloat16),
             pltpu.SemaphoreType.DMA((2, LOCAL_BINS)),
         ],
         compiler_params=pltpu.CompilerParams(vmem_limit_bytes=SCOPE),
-    )(offsets, valid, odd, ready, edge, gather, right)
+    )(offsets, valid, odd, ready, far, edge, gather, right)
 
 
 def per_device(records, partner, valid):
@@ -273,21 +274,31 @@
     gather, own = (jnp.asarray(x) for x in gather_tables())
 
     def fetch(array, even, odd):
-        route = [((c + (odd if c % 2 else even)) % blocks, c) for c in range(blocks)]
-        return lax.ppermute(array, chan, route)
+        source = {c: c + (odd if c % 2 else even) for c in range(blocks)}
+        last = blocks - 1
+        if even == 2:
+            source[1], source[last - 1] = 0, last
+        elif even == 1:
+            pass
+        elif even == -3:
+            source[0], source[2], source[last], source[last - 2] = 2, 0, last - 2, last
+        else:
+            source[0], source[2] = 1, 0
+            source[last], source[last - 2] = last - 1, last
+        return lax.ppermute(array, chan, [(f, c) for c, f in source.items()])
 
     white = whiten(records, table)
     mine = lax.all_to_all(
         white.reshape(2 * TM, ROWS, LANES), ("tm", "side"), 0, 0, tiled=True
     ).reshape(TM, 2, ROWS, LANES)
     near = fetch(mine, -1, 1)
-    far = fetch(mine, 2, -2)
-    edge = fetch(lax.dynamic_index_in_dim(far, side, 1, keepdims=False), -1, 1)
+    edge = fetch(lax.dynamic_index_in_dim(mine, side, 1, keepdims=False), -3, 3)
+    far = fetch(near, 1, -1)
     offsets = partner - (lax.axis_index("pair") * 2 + side)
     odd = side.reshape(1)
     right = spread(odd, mine, own)
-    ready = turn(near, mine, far, gather)
-    result = stack(offsets, valid, odd, ready, edge, gather, right)
+    ready = turn(near, mine, gather)
+    result = stack(offsets, valid, odd, ready, far, edge, gather, right)
     return jnp.transpose(result, (0, 1, 3, 2))
 
 

time: 36.1 us -> 33.3 us (0.922)
  the two profiles are of different devices: /device:TPU:8 before, /device:TPU:6 now
where the time goes in v3:
time: 33.3 us; the launch traced here: 33.2 us
  blocking collectives  12.3 us (37%)
  starting transfers between devices  7.13 us (21%)
  waiting for transfers between devices  7.05 us (21%)
  Pallas kernels  6.63 us (20%)
    all_to_all x1, blocking collectives, per_device(): lax.all_to_all(white.reshape(2 * TM, ROWS, LANES), ('tm', 'side'), 0, 0,...  12.3 us
    ppermute x3, starting transfers between devices, fetch(): return lax.ppermute(array, chan, [(f, c) for c, f in source.items()])  7.13 us
    ppermute x3, waiting for transfers between devices, fetch(): return lax.ppermute(array, chan, [(f, c) for c, f in source.items()])  7.05 us
    pallas_call x1, Pallas kernels, stack(): pl.pallas_call(stack_kernel, in_specs=[scalars] * 3 + [whole] * 5, out_sp...  3 us
    pallas_call x1, Pallas kernels, whiten(): pl.pallas_call(whiten_kernel, in_specs=[pl.BlockSpec(memory_space=pltpu.H...  2.72 us
  transfers between devices with their start and end apart: 3, of which 3 were waited for; matrix products, arithmetic and copies ran while one was open for 0% of the time, Pallas kernels for 3%

profile of v3, /device:TPU:6, one launch (start us, length us, event | category | flops | bytes accessed | tf_op | source)
XLA Modules:
  0.0 33.2 jit_solution(12012260674370143794)
XLA Ops:
  0.0 0.0 copy-start.1
  0.0 0.0 copy-start
  0.0 0.0 copy-start.3
  0.0 2.7 %shard_map.64 = bf16[8,2,32,128]{3,2,1,0:T(8,128)(2,1)S(1)} custom-call(bf16[8,64,3000]{2,1,0:T(8,128)(2,1)} %constant.21.clone.table_hbm, bf16[3,160,3000]{2,1,0:T(8,128)(2,1)} %records_hbm.1), custom_call_target="tpu_custom_call" | custom-call | tf_op jit(solution)/shard_map/pallas_call | solution.py:109
  2.7 0.0 copy-start.2
  2.7 12.3 %all_to_all.5 = bf16[16,32,128]{2,1,0:T(8,128)(2,1)S(1)} all-to-all(bf16[16,32,128]{2,1,0:T(8,128)(2,1)S(1)} %bitcast.10), channel_id=1, replica_groups=mesh['tm'=8,'pair'=16,'side'=2] {'tm','side'}, dimensions={0} | all-to-all | bytes 262144 | tf_op jit(solution)/shard_map/all_to_all | solution.py:291
  15.1 5.0 %collective-permute-start = (bf16[8,2,32,128]{3,2,1,0:T(8,128)(2,1)S(1)}, bf16[8,2,32,128]{3,2,1,0:T(8,128)(2,1)S(1)}, u32[]{:S(2)}, u32[]{:S(2)}) collective-permute-start(bf16[8,2,32,128]{3,2,1,0:T(8,128)(2,1)S(1)} %bitcast.6), channel_id=1, source_target_pairs={{1,0},{2,1},{0,2},{4,3},{3,4},{6,5},{5,6},{8,7},{7,8},{10,9},{9,10... | collective-permute-start | bytes 393224 | tf_op jit(solution)/shard_map/ppermute | solution.py:288
  20.1 2.1 %collective-permute-start.2 = (bf16[8,32,128]{2,1,0:T(8,128)(2,1)S(1)}, bf16[8,32,128]{2,1,0:T(8,128)(2,1)S(1)}, u32[]{:S(2)}, u32[]{:S(2)}) collective-permute-start(bf16[8,32,128]{2,1,0:T(8,128)(2,1)S(1)} %dynamic-slice_bitcast_fusion), channel_id=1, source_target_pairs={{2,0},{4,1},{0,2},{6,3},{1,4},{8,5},{3,6},{10,7},{5,8},{12,9},{7,1... | collective-permute-start | bytes 196616 | tf_op jit(solution)/shard_map/ppermute | solution.py:288
  22.2 3.0 %collective-permute-done.near_ref = bf16[8,2,32,128]{3,2,1,0:T(8,128)(2,1)S(1)} collective-permute-done((bf16[8,2,32,128]{3,2,1,0:T(8,128)(2,1)S(1)}, bf16[8,2,32,128]{3,2,1,0:T(8,128)(2,1)S(1)}, u32[]{:S(2)}, u32[]{:S(2)}) %collective-permute-start) | collective-permute-done | bytes 131104 | tf_op jit(solution)/shard_map/ppermute | solution.py:288
  25.2 0.0 collective-permute-start.1
  25.2 0.0 copy-done.3
  25.2 0.0 copy-done.1
  25.2 0.4 %shard_map.66.right_ref = bf16[4,2,4,64,256]{4,3,2,1,0:T(8,128)(2,1)S(1)} custom-call(s32[1]{0:T(128)} %bitcast.odd_ref, bf16[8,2,32,128]{3,2,1,0:T(8,128)(2,1)S(1)} %bitcast.8, bf16[4,128,256]{2,1,0:T(8,128)(2,1)S(1)} %copy-done.1), custom_call_target="tpu_custom_call" | custom-call | flops 70000000 | bytes 3000000 | tf_op jit(solution)/shard_map/pallas_call | solution.py:148
  25.6 0.0 copy-done
  25.6 0.6 %shard_map.65.ready_ref = bf16[4,2,160,512]{3,2,1,0:T(8,128)(2,1)S(1)} custom-call(bf16[8,2,32,128]{3,2,1,0:T(8,128)(2,1)S(1)} %collective-permute-done.near_ref, bf16[8,2,32,128]{3,2,1,0:T(8,128)(2,1)S(1)} %bitcast.9, bf16[2,256,512]{2,1,0:T(8,128)(2,1)S(1)} %copy-done), custom_call_target="tpu_custom_call" | custom-call | flops 200000000 | bytes 3000000 | tf_op jit(solution)/shard_map/pallas_call | solution.py:182
  26.2 2.2 %collective-permute-done.2.edge_ref = bf16[8,32,128]{2,1,0:T(8,128)(2,1)S(1)} collective-permute-done((bf16[8,32,128]{2,1,0:T(8,128)(2,1)S(1)}, bf16[8,32,128]{2,1,0:T(8,128)(2,1)S(1)}, u32[]{:S(2)}, u32[]{:S(2)}) %collective-permute-start.2) | collective-permute-done | bytes 65568 | tf_op jit(solution)/shard_map/ppermute | solution.py:288
  28.3 1.9 %collective-permute-done.1.far_ref = bf16[8,2,32,128]{3,2,1,0:T(8,128)(2,1)S(1)} collective-permute-done((bf16[8,2,32,128]{3,2,1,0:T(8,128)(2,1)S(1)}, bf16[8,2,32,128]{3,2,1,0:T(8,128)(2,1)S(1)}, u32[]{:S(2)}, u32[]{:S(2)}) %collective-permute-start.1) | collective-permute-done | bytes 131104 | tf_op jit(solution)/shard_map/ppermute | solution.py:288
  30.2 0.0 copy-done.2
  30.2 3.0 %shard_map.67 = bf16[2,4,160,1120]{3,2,1,0:T(8,128)(2,1)} custom-call(s32[1,7]{1,0:T(1,128)S(1)} %broadcast_subtract_fusion.offset_ref, s32[1,7]{1,0:T(1,128)S(1)} %copy-done.2, s32[1]{0:T(128)} %bitcast.odd_ref, bf16[4,2,160,512]{3,2,1,0:T(8,128)(2,1)S(1)} %shard_map.65.ready_ref, bf16[8,2,32,128]{3,2,1,0:T(8,128)(2,1)S(1)} %collective-permute-done.1.far_ref, ...), custom_call_target="tpu_custom_call" | custom-call | tf_op jit(solution)/shard_map/pallas_call | solution.py:255
  (2 shorter events, 0.0 us)
Async XLA Ops:
  0.0 25.2 %copy-start.1 = (bf16[4,128,256]{2,1,0:T(8,128)(2,1)S(1)}, bf16[4,128,256]{2,1,0:T(8,128)(2,1)}, u32[]{:S(2)}) copy-start(bf16[4,128,256]{2,1,0:T(8,128)(2,1)} %constant.23.clone.own_ref) | copy-start | bytes 786436
  0.0 25.6 %copy-start = (bf16[2,256,512]{2,1,0:T(8,128)(2,1)S(1)}, bf16[2,256,512]{2,1,0:T(8,128)(2,1)}, u32[]{:S(2)}) copy-start(bf16[2,256,512]{2,1,0:T(8,128)(2,1)} %constant.22.clone.gather_ref) | copy-start | bytes 1572868
  0.0 25.2 %copy-start.3 = (s32[1,7]{1,0:T(1,128)S(1)}, s32[1,7]{1,0:T(1,128)}, u32[]{:S(2)}) copy-start(s32[1,7]{1,0:T(1,128)} %param.7) | copy-start | bytes 88
  2.7 27.5 %copy-start.2 = (s32[1,7]{1,0:T(1,128)S(1)}, s32[1,7]{1,0:T(1,128)}, u32[]{:S(2)}) copy-start(s32[1,7]{1,0:T(1,128)} %valid_ref.1) | copy-start | bytes 88
  15.1 10.2 %collective-permute-start = (bf16[8,2,32,128]{3,2,1,0:T(8,128)(2,1)S(1)}, bf16[8,2,32,128]{3,2,1,0:T(8,128)(2,1)S(1)}, u32[]{:S(2)}, u32[]{:S(2)}) collective-permute-start(bf16[8,2,32,128]{3,2,1,0:T(8,128)(2,1)S(1)} %bitcast.6), channel_id=1, source_target_pairs={{1,0},{2,1},{0,2},{4,3},{3,4},{6,5},{5,6},{8,7},{7,8},{10,9},{9,10... | collective-permute-start | bytes 393224 | tf_op jit(solution)/shard_map/ppermute | solution.py:288
  20.1 8.2 %collective-permute-start.2 = (bf16[8,32,128]{2,1,0:T(8,128)(2,1)S(1)}, bf16[8,32,128]{2,1,0:T(8,128)(2,1)S(1)}, u32[]{:S(2)}, u32[]{:S(2)}) collective-permute-start(bf16[8,32,128]{2,1,0:T(8,128)(2,1)S(1)} %dynamic-slice_bitcast_fusion), channel_id=1, source_target_pairs={{2,0},{4,1},{0,2},{6,3},{1,4},{8,5},{3,6},{10,7},{5,8},{12,9},{7,1... | collective-permute-start | bytes 196616 | tf_op jit(solution)/shard_map/ppermute | solution.py:288
  25.2 5.0 %collective-permute-start.1 = (bf16[8,2,32,128]{3,2,1,0:T(8,128)(2,1)S(1)}, bf16[8,2,32,128]{3,2,1,0:T(8,128)(2,1)S(1)}, u32[]{:S(2)}, u32[]{:S(2)}) collective-permute-start(bf16[8,2,32,128]{3,2,1,0:T(8,128)(2,1)S(1)} %collective-permute-done.near_ref), channel_id=1, source_target_pairs={{1,0},{0,1},{3,2},{2,3},{5,4},{4,5},{7,6},{6,7},{9,8},{8,9},{11,10... | collective-permute-start | bytes 393224 | tf_op jit(solution)/shard_map/ppermute | solution.py:288

commit v4 on v3

--- a/solution.py
+++ b/solution.py
@@ -120,8 +120,10 @@
     )(table, records)
 
 
-def spread_kernel(odd_ref, mine_ref, own_ref, out_ref):
-    own = jnp.where(odd_ref[0] == 1, mine_ref[:, 1], mine_ref[:, 0]).reshape(TM * ROWS, LANES)
+def spread_kernel(odd_ref, mine_ref, own_ref, out_ref, alone_ref):
+    alone = jnp.where(odd_ref[0] == 1, mine_ref[:, 1], mine_ref[:, 0])
+    alone_ref[...] = alone
+    own = alone.reshape(TM * ROWS, LANES)
     lane = lax.broadcasted_iota(jnp.int32, (USED, LANES), 1)
     fill = jnp.zeros((DEPTH - USED, LANES), jnp.bfloat16)
     for f in range(LOCAL_BINS):
@@ -149,8 +151,11 @@
         spread_kernel,
         in_specs=[pl.BlockSpec(memory_space=pltpu.SMEM)]
         + [pl.BlockSpec(memory_space=pltpu.VMEM)] * 2,
-        out_specs=pl.BlockSpec(memory_space=pltpu.VMEM),
-        out_shape=jax.ShapeDtypeStruct(shape, jnp.bfloat16),
+        out_specs=[pl.BlockSpec(memory_space=pltpu.VMEM)] * 2,
+        out_shape=[
+            jax.ShapeDtypeStruct(shape, jnp.bfloat16),
+            jax.ShapeDtypeStruct((TM, ROWS, LANES), jnp.bfloat16),
+        ],
         compiler_params=pltpu.CompilerParams(vmem_limit_bytes=SCOPE),
         cost_estimate=pl.CostEstimate(flops=70_000_000, bytes_accessed=3_000_000, transcendentals=0),
     )(odd, mine, own)
@@ -169,48 +174,45 @@
     return jnp.concatenate([whole, last], 0).astype(jnp.bfloat16)
 
 
-def turn_kernel(near_ref, mine_ref, gather_ref, out_ref):
-    for n, ref in enumerate((near_ref, mine_ref)):
-        for i in range(2):
-            block = ref[:, i].reshape(TM * ROWS, LANES)
-            for order in range(2):
-                out_ref[2 * n + i, order] = turned(block, gather_ref[order])
-
-
-def turn(near, mine, gather):
-    shape = (4, 2, WIDTH, LOCAL_BINS * LANES)
-    return pl.pallas_call(
-        turn_kernel,
-        in_specs=[pl.BlockSpec(memory_space=pltpu.VMEM)] * 3,
-        out_specs=pl.BlockSpec(memory_space=pltpu.VMEM),
-        out_shape=jax.ShapeDtypeStruct(shape, jnp.bfloat16),
-        compiler_params=pltpu.CompilerParams(vmem_limit_bytes=SCOPE),
-        cost_estimate=pl.CostEstimate(flops=200_000_000, bytes_accessed=3_000_000, transcendentals=0),
-    )(near, mine, gather)
-
-
-def stack_kernel(
-    offset_ref, valid_ref, odd_ref, ready_ref, far_ref, edge_ref, gather_ref, right_ref, out_hbm,
-    last_ref, out_ref, sems,
-):
-    odd = odd_ref[0]
-    for n, block in enumerate((far_ref[:, 0], far_ref[:, 1], edge_ref[...])):
-        for order in range(2):
-            last_ref[n, order] = turned(block.reshape(TM * ROWS, LANES), gather_ref[order])
-    places = []
-    for p in range(SLOTS):
-        d = offset_ref[0, p]
-        at_even = jnp.where(d == -3, 6, d + 2)
-        at_odd = jnp.where(
-            d == 3, 6, jnp.where(d <= -2, d + 7, jnp.where(d <= 0, d + 3, d - 1))
-        )
-        places.append(jnp.where(odd == 1, at_odd, at_even))
+def turn_kernel(valid_ref, near_ref, mine_ref, gather_ref, out_ref, weight_ref):
     column = lax.broadcasted_iota(jnp.int32, (1, 2 * SPAN), 1)
     weight = jnp.zeros((1, 2 * SPAN), jnp.float32)
     for p in range(SLOTS):
         here = (column >= WIDTH * p) & (column < WIDTH * (p + 1))
         weight = jnp.where(here, valid_ref[0, p].astype(jnp.float32), weight)
     weight = weight * (1.0 / math.sqrt(SEG_LOCAL * TM))
+    weight_ref[...] = weight
+    for n, ref in enumerate((near_ref, mine_ref)):
+        for i in range(2):
+            block = ref[:, i].reshape(TM * ROWS, LANES)
+            for order in range(2):
+                out_ref[2 * n + i, order] = turned(block, gather_ref[order])
+
+
+def turn(valid, near, mine, gather):
+    shape = (4, 2, WIDTH, LOCAL_BINS * LANES)
+    return pl.pallas_call(
+        turn_kernel,
+        in_specs=[pl.BlockSpec(memory_space=pltpu.VMEM)] * 4,
+        out_specs=[pl.BlockSpec(memory_space=pltpu.VMEM)] * 2,
+        out_shape=[
+            jax.ShapeDtypeStruct(shape, jnp.bfloat16),
+            jax.ShapeDtypeStruct((1, 2 * SPAN), jnp.float32),
+        ],
+        compiler_params=pltpu.CompilerParams(vmem_limit_bytes=SCOPE),
+        cost_estimate=pl.CostEstimate(flops=200_000_000, bytes_accessed=3_000_000, transcendentals=0),
+    )(valid, near, mine, gather)
+
+
+def stack_kernel(
+    places_ref, weight_ref, ready_ref, far_ref, edge_ref, gather_ref, right_ref, out_hbm,
+    last_ref, out_ref, sems,
+):
+    places = [places_ref[0, p] for p in range(SLOTS)]
+    for n, block in enumerate((far_ref[:, 0], far_ref[:, 1], edge_ref[...])):
+        for order in range(2):
+            last_ref[n, order] = turned(block.reshape(TM * ROWS, LANES), gather_ref[order])
+    weight = weight_ref[...]
     zero = jnp.zeros((DEPTH, LANES), jnp.bfloat16)
     copies = []
     for f in range(LOCAL_BINS):
@@ -248,13 +250,12 @@
         copy.wait()
 
 
-def stack(offsets, valid, odd, ready, far, edge, gather, right):
+def stack(places, weight, ready, far, edge, gather, right):
     whole = pl.BlockSpec(memory_space=pltpu.VMEM)
-    scalars = pl.BlockSpec(memory_space=pltpu.SMEM)
     shape = (2, LOCAL_BINS, WIDTH, SLOTS * WIDTH)
     return pl.pallas_call(
         stack_kernel,
-        in_specs=[scalars] * 3 + [whole] * 5,
+        in_specs=[whole] * 7,
         out_specs=pl.BlockSpec(memory_space=pltpu.HBM),
         out_shape=jax.ShapeDtypeStruct(shape, jnp.bfloat16),
         scratch_shapes=[
@@ -263,7 +264,14 @@
             pltpu.SemaphoreType.DMA((2, LOCAL_BINS)),
         ],
         compiler_params=pltpu.CompilerParams(vmem_limit_bytes=SCOPE),
-    )(offsets, valid, odd, ready, far, edge, gather, right)
+    )(places, weight, ready, far, edge, gather, right)
+
+
+def place_of(partner, me, side):
+    d = partner - me
+    at_even = jnp.where(d == -3, 6, d + 2)
+    at_odd = jnp.where(d == 3, 6, jnp.where(d <= -2, d + 7, jnp.where(d <= 0, d + 3, d - 1)))
+    return jnp.where(side == 1, at_odd, at_even)
 
 
 def per_device(records, partner, valid):
@@ -292,13 +300,13 @@
         white.reshape(2 * TM, ROWS, LANES), ("tm", "side"), 0, 0, tiled=True
     ).reshape(TM, 2, ROWS, LANES)
     near = fetch(mine, -1, 1)
-    edge = fetch(lax.dynamic_index_in_dim(mine, side, 1, keepdims=False), -3, 3)
+    odd = side.reshape(1)
+    right, alone = spread(odd, mine, own)
+    edge = fetch(alone, -3, 3)
     far = fetch(near, 1, -1)
-    offsets = partner - (lax.axis_index("pair") * 2 + side)
-    odd = side.reshape(1)
-    right = spread(odd, mine, own)
-    ready = turn(near, mine, gather)
-    result = stack(offsets, valid, odd, ready, far, edge, gather, right)
+    me = lax.axis_index("pair") * 2 + side
+    ready, weight = turn(valid, near, mine, gather)
+    result = stack(place_of(partner, me, side), weight, ready, far, edge, gather, right)
     return jnp.transpose(result, (0, 1, 3, 2))
 
 

time: 33.3 us -> 32.4 us (0.973)
  Pallas kernels: 6.63 us -> 6.09 us
  waiting for transfers between devices: 7.05 us -> 6.6 us
    pallas_call x1, Pallas kernels: 3 us -> 2.47 us  [stack(): pl.pallas_call(stack_kernel, in_specs=[whole] * 7, out_specs=pl.BlockSpec...]
    ppermute x3, waiting for transfers between devices: 7.05 us -> 6.6 us  [fetch(): return lax.ppermute(array, chan, [(f, c) for c, f in source.items()])]
where the time goes in v4:
time: 32.4 us; the launch traced here: 32.3 us
  blocking collectives  12.3 us (38%)
  starting transfers between devices  7.22 us (22%)
  waiting for transfers between devices  6.6 us (20%)
  Pallas kernels  6.09 us (19%)
    all_to_all x1, blocking collectives, per_device(): lax.all_to_all(white.reshape(2 * TM, ROWS, LANES), ('tm', 'side'), 0, 0,...  12.3 us
    ppermute x3, starting transfers between devices, fetch(): return lax.ppermute(array, chan, [(f, c) for c, f in source.items()])  7.22 us
    ppermute x3, waiting for transfers between devices, fetch(): return lax.ppermute(array, chan, [(f, c) for c, f in source.items()])  6.6 us
    pallas_call x1, Pallas kernels, whiten(): pl.pallas_call(whiten_kernel, in_specs=[pl.BlockSpec(memory_space=pltpu.H...  2.71 us
    pallas_call x1, Pallas kernels, stack(): pl.pallas_call(stack_kernel, in_specs=[whole] * 7, out_specs=pl.BlockSpec...  2.47 us
  transfers between devices with their start and end apart: 3, of which 3 were waited for; matrix products, arithmetic and copies ran while one was open for 0% of the time, Pallas kernels for 3%

profile of v4, /device:TPU:6, one launch (start us, length us, event | category | flops | bytes accessed | tf_op | source)
XLA Modules:
  0.0 32.3 jit_solution(4511955897054008311)
XLA Ops:
  0.0 0.0 copy-start.1
  0.0 0.0 copy-start
  0.0 0.0 copy-start.3
  0.0 0.0 copy-start.2
  0.0 2.7 %shard_map.64 = bf16[8,2,32,128]{3,2,1,0:T(8,128)(2,1)S(1)} custom-call(bf16[8,64,3000]{2,1,0:T(8,128)(2,1)} %constant.34.clone.table_hbm, bf16[3,160,3000]{2,1,0:T(8,128)(2,1)} %records_hbm.1), custom_call_target="tpu_custom_call" | custom-call | tf_op jit(solution)/shard_map/pallas_call | solution.py:109
  2.7 12.3 %all_to_all.5 = bf16[16,32,128]{2,1,0:T(8,128)(2,1)S(1)} all-to-all(bf16[16,32,128]{2,1,0:T(8,128)(2,1)S(1)} %bitcast.7), channel_id=1, replica_groups=mesh['tm'=8,'pair'=16,'side'=2] {'tm','side'}, dimensions={0} | all-to-all | bytes 262144 | tf_op jit(solution)/shard_map/all_to_all | solution.py:299
  15.1 5.0 %collective-permute-start = (bf16[8,2,32,128]{3,2,1,0:T(8,128)(2,1)S(1)}, bf16[8,2,32,128]{3,2,1,0:T(8,128)(2,1)S(1)}, u32[]{:S(2)}, u32[]{:S(2)}) collective-permute-start(bf16[8,2,32,128]{3,2,1,0:T(8,128)(2,1)S(1)} %bitcast.4), channel_id=1, source_target_pairs={{1,0},{2,1},{0,2},{4,3},{3,4},{6,5},{5,6},{8,7},{7,8},{10,9},{9,10... | collective-permute-start | bytes 393224 | tf_op jit(solution)/shard_map/ppermute | solution.py:296
  20.1 0.0 copy-done.1
  20.1 0.4 %shard_map.66 = (bf16[4,2,4,64,256]{4,3,2,1,0:T(8,128)(2,1)S(1)}, bf16[8,32,128]{2,1,0:T(8,128)(2,1)S(1)}) custom-call(s32[1]{0:T(128)} %bitcast.2.odd_ref, bf16[8,2,32,128]{3,2,1,0:T(8,128)(2,1)S(1)} %bitcast.5, bf16[4,128,256]{2,1,0:T(8,128)(2,1)S(1)} %copy-done.1), custom_call_target="tpu_custom_call" | custom-call | flops 70000000 | bytes 3000000 | tf_op jit(solution)/shard_map/pallas_call | solution.py:150
  20.4 2.2 %collective-permute-start.2 = (bf16[8,32,128]{2,1,0:T(8,128)(2,1)S(1)}, bf16[8,32,128]{2,1,0:T(8,128)(2,1)S(1)}, u32[]{:S(2)}, u32[]{:S(2)}) collective-permute-start(bf16[8,32,128]{2,1,0:T(8,128)(2,1)S(1)} %get-tuple-element.11), channel_id=1, source_target_pairs={{2,0},{4,1},{0,2},{6,3},{1,4},{8,5},{3,6},{10,7},{5,8},{12,9},{7,1... | collective-permute-start | bytes 196616 | tf_op jit(solution)/shard_map/ppermute | solution.py:296
  22.6 2.2 %collective-permute-done.near_ref = bf16[8,2,32,128]{3,2,1,0:T(8,128)(2,1)S(1)} collective-permute-done((bf16[8,2,32,128]{3,2,1,0:T(8,128)(2,1)S(1)}, bf16[8,2,32,128]{3,2,1,0:T(8,128)(2,1)S(1)}, u32[]{:S(2)}, u32[]{:S(2)}) %collective-permute-start) | collective-permute-done | bytes 131104 | tf_op jit(solution)/shard_map/ppermute | solution.py:296
  24.9 0.0 collective-permute-start.1
  24.9 0.0 copy-done.3
  24.9 0.0 copy-done
  24.9 0.0 copy-done.2
  24.9 0.6 %shard_map.65 = (bf16[4,2,160,512]{3,2,1,0:T(8,128)(2,1)S(1)}, f32[1,1280]{1,0:T(1,128)S(1)}) custom-call(s32[1,7]{1,0:T(1,128)S(1)} %copy-done.2, bf16[8,2,32,128]{3,2,1,0:T(8,128)(2,1)S(1)} %collective-permute-done.near_ref, bf16[8,2,32,128]{3,2,1,0:T(8,128)(2,1)S(1)} %bitcast.6, bf16[2,256,512]{2,1,0:T(8,128)(2,1)S(1)} %copy-done), custom_call_target="tpu_custom_call" | custom-call | flops 200000000 | bytes 3000000 | tf_op jit(solution)/shard_map/pallas_call | solution.py:194
  25.5 3.5 %collective-permute-done.2.edge_ref = bf16[8,32,128]{2,1,0:T(8,128)(2,1)S(1)} collective-permute-done((bf16[8,32,128]{2,1,0:T(8,128)(2,1)S(1)}, bf16[8,32,128]{2,1,0:T(8,128)(2,1)S(1)}, u32[]{:S(2)}, u32[]{:S(2)}) %collective-permute-start.2) | collective-permute-done | bytes 65568 | tf_op jit(solution)/shard_map/ppermute | solution.py:296
  28.9 0.9 %collective-permute-done.1.far_ref = bf16[8,2,32,128]{3,2,1,0:T(8,128)(2,1)S(1)} collective-permute-done((bf16[8,2,32,128]{3,2,1,0:T(8,128)(2,1)S(1)}, bf16[8,2,32,128]{3,2,1,0:T(8,128)(2,1)S(1)}, u32[]{:S(2)}, u32[]{:S(2)}) %collective-permute-start.1) | collective-permute-done | bytes 131104 | tf_op jit(solution)/shard_map/ppermute | solution.py:296
  29.8 2.5 %shard_map.67 = bf16[2,4,160,1120]{3,2,1,0:T(8,128)(2,1)} custom-call(s32[1,7]{1,0:T(1,128)S(1)} %broadcast_select_fusion.places_ref, f32[1,1280]{1,0:T(1,128)S(1)} %get-tuple-element.9.weight_ref, bf16[4,2,160,512]{3,2,1,0:T(8,128)(2,1)S(1)} %get-tuple-element.10.ready_ref, bf16[8,2,32,128]{3,2,1,0:T(8,128)(2,1)S(1)} %collective-permute-done.1.far_ref, ...), custom_call_target="tpu_custom_call" | custom-call | tf_op jit(solution)/shard_map/pallas_call | solution.py:256
  (1 shorter events, 0.0 us)
Async XLA Ops:
  0.0 20.1 %copy-start.1 = (bf16[4,128,256]{2,1,0:T(8,128)(2,1)S(1)}, bf16[4,128,256]{2,1,0:T(8,128)(2,1)}, u32[]{:S(2)}) copy-start(bf16[4,128,256]{2,1,0:T(8,128)(2,1)} %constant.36.clone.own_ref) | copy-start | bytes 786436
  0.0 24.9 %copy-start = (bf16[2,256,512]{2,1,0:T(8,128)(2,1)S(1)}, bf16[2,256,512]{2,1,0:T(8,128)(2,1)}, u32[]{:S(2)}) copy-start(bf16[2,256,512]{2,1,0:T(8,128)(2,1)} %constant.35.clone.gather_ref) | copy-start | bytes 1572868
  0.0 24.9 %copy-start.3 = (s32[1,7]{1,0:T(1,128)S(1)}, s32[1,7]{1,0:T(1,128)}, u32[]{:S(2)}) copy-start(s32[1,7]{1,0:T(1,128)} %param.7) | copy-start | bytes 88
  0.0 24.9 %copy-start.2 = (s32[1,7]{1,0:T(1,128)S(1)}, s32[1,7]{1,0:T(1,128)}, u32[]{:S(2)}) copy-start(s32[1,7]{1,0:T(1,128)} %valid_ref.1) | copy-start | bytes 88
  15.1 9.8 %collective-permute-start = (bf16[8,2,32,128]{3,2,1,0:T(8,128)(2,1)S(1)}, bf16[8,2,32,128]{3,2,1,0:T(8,128)(2,1)S(1)}, u32[]{:S(2)}, u32[]{:S(2)}) collective-permute-start(bf16[8,2,32,128]{3,2,1,0:T(8,128)(2,1)S(1)} %bitcast.4), channel_id=1, source_target_pairs={{1,0},{2,1},{0,2},{4,3},{3,4},{6,5},{5,6},{8,7},{7,8},{10,9},{9,10... | collective-permute-start | bytes 393224 | tf_op jit(solution)/shard_map/ppermute | solution.py:296
  20.4 8.5 %collective-permute-start.2 = (bf16[8,32,128]{2,1,0:T(8,128)(2,1)S(1)}, bf16[8,32,128]{2,1,0:T(8,128)(2,1)S(1)}, u32[]{:S(2)}, u32[]{:S(2)}) collective-permute-start(bf16[8,32,128]{2,1,0:T(8,128)(2,1)S(1)} %get-tuple-element.11), channel_id=1, source_target_pairs={{2,0},{4,1},{0,2},{6,3},{1,4},{8,5},{3,6},{10,7},{5,8},{12,9},{7,1... | collective-permute-start | bytes 196616 | tf_op jit(solution)/shard_map/ppermute | solution.py:296
  24.9 5.0 %collective-permute-start.1 = (bf16[8,2,32,128]{3,2,1,0:T(8,128)(2,1)S(1)}, bf16[8,2,32,128]{3,2,1,0:T(8,128)(2,1)S(1)}, u32[]{:S(2)}, u32[]{:S(2)}) collective-permute-start(bf16[8,2,32,128]{3,2,1,0:T(8,128)(2,1)S(1)} %collective-permute-done.near_ref), channel_id=1, source_target_pairs={{1,0},{0,1},{3,2},{2,3},{5,4},{4,5},{7,6},{6,7},{9,8},{8,9},{11,10... | collective-permute-start | bytes 393224 | tf_op jit(solution)/shard_map/ppermute | solution.py:296

commit v5 on v4

--- a/solution.py
+++ b/solution.py
@@ -69,19 +69,23 @@
     copies = []
     for i, cut in enumerate(cuts):
         part = pl.ds(cut.start, cut.stop - cut.start)
-        if i == 0:
-            copies.append(pltpu.make_async_copy(table_hbm.at[0], table_ref, sems.at[len(cuts)]))
         copies.append(
-            pltpu.make_async_copy(
-                records_hbm.at[:, :, part], records_ref.at[:, :, part], sems.at[i]
+            (
+                pltpu.make_async_copy(
+                    table_hbm.at[0, :, part], table_ref.at[:, part], sems.at[i, 0]
+                ),
+                pltpu.make_async_copy(
+                    records_hbm.at[:, :, part], records_ref.at[:, :, part], sems.at[i, 1]
+                ),
             )
         )
-    for copy in copies:
-        copy.start()
-    copies[0].wait()
+    for pair in copies:
+        for copy in pair:
+            copy.start()
     total = None
     for i, cut in enumerate(cuts):
-        copies[i + 1].wait()
+        for copy in copies[i]:
+            copy.wait()
         product = lax.dot_general(
             table_ref[:, cut],
             records_ref[:, :, cut].reshape(SEG_LOCAL * WIDTH, cut.stop - cut.start),
@@ -114,7 +118,7 @@
         scratch_shapes=[
             pltpu.VMEM(table.shape[1:], jnp.bfloat16),
             pltpu.VMEM(records.shape, jnp.bfloat16),
-            pltpu.SemaphoreType.DMA((cuts + 1,)),
+            pltpu.SemaphoreType.DMA((cuts, 2)),
         ],
         compiler_params=pltpu.CompilerParams(vmem_limit_bytes=WHOLE),
     )(table, records)

time: 32.4 us -> 32.4 us (level)
  no operation moved by 1% of the time
where the time goes in v5:
time: 32.4 us; the launch traced here: 32.3 us
  blocking collectives  12.3 us (38%)
  starting transfers between devices  7.22 us (22%)
  waiting for transfers between devices  6.6 us (20%)
  Pallas kernels  6.08 us (19%)
    all_to_all x1, blocking collectives, per_device(): lax.all_to_all(white.reshape(2 * TM, ROWS, LANES), ('tm', 'side'), 0, 0,...  12.3 us
    ppermute x3, starting transfers between devices, fetch(): return lax.ppermute(array, chan, [(f, c) for c, f in source.items()])  7.22 us
    ppermute x3, waiting for transfers between devices, fetch(): return lax.ppermute(array, chan, [(f, c) for c, f in source.items()])  6.6 us
    pallas_call x1, Pallas kernels, whiten(): pl.pallas_call(whiten_kernel, in_specs=[pl.BlockSpec(memory_space=pltpu.H...  2.69 us
    pallas_call x1, Pallas kernels, stack(): pl.pallas_call(stack_kernel, in_specs=[whole] * 7, out_specs=pl.BlockSpec...  2.47 us
  transfers between devices with their start and end apart: 3, of which 3 were waited for; matrix products, arithmetic and copies ran while one was open for 0% of the time, Pallas kernels for 3%

profile of v5, /device:TPU:6, one launch (start us, length us, event | category | flops | bytes accessed | tf_op | source)
XLA Modules:
  0.0 32.3 jit_solution(6756470651370004263)
XLA Ops:
  0.0 0.0 copy-start.1
  0.0 0.0 copy-start
  0.0 0.0 copy-start.3
  0.0 0.0 copy-start.2
  0.0 2.7 %shard_map.64 = bf16[8,2,32,128]{3,2,1,0:T(8,128)(2,1)S(1)} custom-call(bf16[8,64,3000]{2,1,0:T(8,128)(2,1)} %constant.34.clone.table_hbm, bf16[3,160,3000]{2,1,0:T(8,128)(2,1)} %records_hbm.1), custom_call_target="tpu_custom_call" | custom-call | tf_op jit(solution)/shard_map/pallas_call | solution.py:113
  2.7 12.3 %all_to_all.5 = bf16[16,32,128]{2,1,0:T(8,128)(2,1)S(1)} all-to-all(bf16[16,32,128]{2,1,0:T(8,128)(2,1)S(1)} %bitcast.7), channel_id=1, replica_groups=mesh['tm'=8,'pair'=16,'side'=2] {'tm','side'}, dimensions={0} | all-to-all | bytes 262144 | tf_op jit(solution)/shard_map/all_to_all | solution.py:303
  15.0 5.0 %collective-permute-start = (bf16[8,2,32,128]{3,2,1,0:T(8,128)(2,1)S(1)}, bf16[8,2,32,128]{3,2,1,0:T(8,128)(2,1)S(1)}, u32[]{:S(2)}, u32[]{:S(2)}) collective-permute-start(bf16[8,2,32,128]{3,2,1,0:T(8,128)(2,1)S(1)} %bitcast.4), channel_id=1, source_target_pairs={{1,0},{2,1},{0,2},{4,3},{3,4},{6,5},{5,6},{8,7},{7,8},{10,9},{9,10... | collective-permute-start | bytes 393224 | tf_op jit(solution)/shard_map/ppermute | solution.py:300
  20.1 0.0 copy-done.1
  20.1 0.4 %shard_map.66 = (bf16[4,2,4,64,256]{4,3,2,1,0:T(8,128)(2,1)S(1)}, bf16[8,32,128]{2,1,0:T(8,128)(2,1)S(1)}) custom-call(s32[1]{0:T(128)} %bitcast.2.odd_ref, bf16[8,2,32,128]{3,2,1,0:T(8,128)(2,1)S(1)} %bitcast.5, bf16[4,128,256]{2,1,0:T(8,128)(2,1)S(1)} %copy-done.1), custom_call_target="tpu_custom_call" | custom-call | flops 70000000 | bytes 3000000 | tf_op jit(solution)/shard_map/pallas_call | solution.py:154
  20.4 2.2 %collective-permute-start.2 = (bf16[8,32,128]{2,1,0:T(8,128)(2,1)S(1)}, bf16[8,32,128]{2,1,0:T(8,128)(2,1)S(1)}, u32[]{:S(2)}, u32[]{:S(2)}) collective-permute-start(bf16[8,32,128]{2,1,0:T(8,128)(2,1)S(1)} %get-tuple-element.11), channel_id=1, source_target_pairs={{2,0},{4,1},{0,2},{6,3},{1,4},{8,5},{3,6},{10,7},{5,8},{12,9},{7,1... | collective-permute-start | bytes 196616 | tf_op jit(solution)/shard_map/ppermute | solution.py:300
  22.6 2.2 %collective-permute-done.near_ref = bf16[8,2,32,128]{3,2,1,0:T(8,128)(2,1)S(1)} collective-permute-done((bf16[8,2,32,128]{3,2,1,0:T(8,128)(2,1)S(1)}, bf16[8,2,32,128]{3,2,1,0:T(8,128)(2,1)S(1)}, u32[]{:S(2)}, u32[]{:S(2)}) %collective-permute-start) | collective-permute-done | bytes 131104 | tf_op jit(solution)/shard_map/ppermute | solution.py:300
  24.9 0.0 collective-permute-start.1
  24.9 0.0 copy-done.3
  24.9 0.0 copy-done
  24.9 0.0 copy-done.2
  24.9 0.6 %shard_map.65 = (bf16[4,2,160,512]{3,2,1,0:T(8,128)(2,1)S(1)}, f32[1,1280]{1,0:T(1,128)S(1)}) custom-call(s32[1,7]{1,0:T(1,128)S(1)} %copy-done.2, bf16[8,2,32,128]{3,2,1,0:T(8,128)(2,1)S(1)} %collective-permute-done.near_ref, bf16[8,2,32,128]{3,2,1,0:T(8,128)(2,1)S(1)} %bitcast.6, bf16[2,256,512]{2,1,0:T(8,128)(2,1)S(1)} %copy-done), custom_call_target="tpu_custom_call" | custom-call | flops 200000000 | bytes 3000000 | tf_op jit(solution)/shard_map/pallas_call | solution.py:198
  25.5 3.5 %collective-permute-done.2.edge_ref = bf16[8,32,128]{2,1,0:T(8,128)(2,1)S(1)} collective-permute-done((bf16[8,32,128]{2,1,0:T(8,128)(2,1)S(1)}, bf16[8,32,128]{2,1,0:T(8,128)(2,1)S(1)}, u32[]{:S(2)}, u32[]{:S(2)}) %collective-permute-start.2) | collective-permute-done | bytes 65568 | tf_op jit(solution)/shard_map/ppermute | solution.py:300
  28.9 0.9 %collective-permute-done.1.far_ref = bf16[8,2,32,128]{3,2,1,0:T(8,128)(2,1)S(1)} collective-permute-done((bf16[8,2,32,128]{3,2,1,0:T(8,128)(2,1)S(1)}, bf16[8,2,32,128]{3,2,1,0:T(8,128)(2,1)S(1)}, u32[]{:S(2)}, u32[]{:S(2)}) %collective-permute-start.1) | collective-permute-done | bytes 131104 | tf_op jit(solution)/shard_map/ppermute | solution.py:300
  29.8 2.5 %shard_map.67 = bf16[2,4,160,1120]{3,2,1,0:T(8,128)(2,1)} custom-call(s32[1,7]{1,0:T(1,128)S(1)} %broadcast_select_fusion.places_ref, f32[1,1280]{1,0:T(1,128)S(1)} %get-tuple-element.9.weight_ref, bf16[4,2,160,512]{3,2,1,0:T(8,128)(2,1)S(1)} %get-tuple-element.10.ready_ref, bf16[8,2,32,128]{3,2,1,0:T(8,128)(2,1)S(1)} %collective-permute-done.1.far_ref, ...), custom_call_target="tpu_custom_call" | custom-call | tf_op jit(solution)/shard_map/pallas_call | solution.py:260
  (1 shorter events, 0.0 us)
Async XLA Ops:
  0.0 20.1 %copy-start.1 = (bf16[4,128,256]{2,1,0:T(8,128)(2,1)S(1)}, bf16[4,128,256]{2,1,0:T(8,128)(2,1)}, u32[]{:S(2)}) copy-start(bf16[4,128,256]{2,1,0:T(8,128)(2,1)} %constant.36.clone.own_ref) | copy-start | bytes 786436
  0.0 24.9 %copy-start = (bf16[2,256,512]{2,1,0:T(8,128)(2,1)S(1)}, bf16[2,256,512]{2,1,0:T(8,128)(2,1)}, u32[]{:S(2)}) copy-start(bf16[2,256,512]{2,1,0:T(8,128)(2,1)} %constant.35.clone.gather_ref) | copy-start | bytes 1572868
  0.0 24.9 %copy-start.3 = (s32[1,7]{1,0:T(1,128)S(1)}, s32[1,7]{1,0:T(1,128)}, u32[]{:S(2)}) copy-start(s32[1,7]{1,0:T(1,128)} %param.7) | copy-start | bytes 88
  0.0 24.9 %copy-start.2 = (s32[1,7]{1,0:T(1,128)S(1)}, s32[1,7]{1,0:T(1,128)}, u32[]{:S(2)}) copy-start(s32[1,7]{1,0:T(1,128)} %valid_ref.1) | copy-start | bytes 88
  15.0 9.8 %collective-permute-start = (bf16[8,2,32,128]{3,2,1,0:T(8,128)(2,1)S(1)}, bf16[8,2,32,128]{3,2,1,0:T(8,128)(2,1)S(1)}, u32[]{:S(2)}, u32[]{:S(2)}) collective-permute-start(bf16[8,2,32,128]{3,2,1,0:T(8,128)(2,1)S(1)} %bitcast.4), channel_id=1, source_target_pairs={{1,0},{2,1},{0,2},{4,3},{3,4},{6,5},{5,6},{8,7},{7,8},{10,9},{9,10... | collective-permute-start | bytes 393224 | tf_op jit(solution)/shard_map/ppermute | solution.py:300
  20.4 8.5 %collective-permute-start.2 = (bf16[8,32,128]{2,1,0:T(8,128)(2,1)S(1)}, bf16[8,32,128]{2,1,0:T(8,128)(2,1)S(1)}, u32[]{:S(2)}, u32[]{:S(2)}) collective-permute-start(bf16[8,32,128]{2,1,0:T(8,128)(2,1)S(1)} %get-tuple-element.11), channel_id=1, source_target_pairs={{2,0},{4,1},{0,2},{6,3},{1,4},{8,5},{3,6},{10,7},{5,8},{12,9},{7,1... | collective-permute-start | bytes 196616 | tf_op jit(solution)/shard_map/ppermute | solution.py:300
  24.9 5.0 %collective-permute-start.1 = (bf16[8,2,32,128]{3,2,1,0:T(8,128)(2,1)S(1)}, bf16[8,2,32,128]{3,2,1,0:T(8,128)(2,1)S(1)}, u32[]{:S(2)}, u32[]{:S(2)}) collective-permute-start(bf16[8,2,32,128]{3,2,1,0:T(8,128)(2,1)S(1)} %collective-permute-done.near_ref), channel_id=1, source_target_pairs={{1,0},{0,1},{3,2},{2,3},{5,4},{4,5},{7,6},{6,7},{9,8},{8,9},{11,10... | collective-permute-start | bytes 393224 | tf_op jit(solution)/shard_map/ppermute | solution.py:300

commit v6 on v5

--- a/solution.py
+++ b/solution.py
@@ -233,14 +233,16 @@
         left = jnp.concatenate(
             [jnp.concatenate(tiles[:2], 1), jnp.concatenate(tiles[2:], 1)], 0
         )
+        rows = []
+        for j in range(4):
+            here = []
+            for part in range(2):
+                pair = [right_ref[f, part, j, :, :LANES], right_ref[f, part, j, :, LANES:]]
+                here += [zero] * j + pair + [zero] * (3 - j)
+            rows.append(jnp.concatenate(here, 1))
+        products = jnp.dot(left, jnp.concatenate(rows, 0), preferred_element_type=jnp.float32)
         for part in range(2):
-            rows = []
-            for j in range(4):
-                here = [right_ref[f, part, j, :, :LANES], right_ref[f, part, j, :, LANES:]]
-                rows.append(jnp.concatenate([zero] * j + here + [zero] * (3 - j), 1))
-            product = jnp.dot(
-                left, jnp.concatenate(rows, 0), preferred_element_type=jnp.float32
-            )
+            product = products[:, SPAN * part : SPAN * (part + 1)]
             out_ref[part, f, :, :SPAN] = (product[:WIDTH] * weight[:, :SPAN]).astype(jnp.bfloat16)
             out_ref[part, f, :, SPAN:] = (
                 product[WIDTH:, : SLOTS * WIDTH - SPAN] * weight[:, SPAN : SLOTS * WIDTH]

time: 32.4 us -> 32.4 us (level)
  no operation moved by 1% of the time
where the time goes in v6:
time: 32.4 us; the launch traced here: 32.2 us
  blocking collectives  12.3 us (38%)
  starting transfers between devices  7.22 us (22%)
  waiting for transfers between devices  6.6 us (20%)
  Pallas kernels  6.04 us (19%)
    all_to_all x1, blocking collectives, per_device(): lax.all_to_all(white.reshape(2 * TM, ROWS, LANES), ('tm', 'side'), 0, 0,...  12.3 us
    ppermute x3, starting transfers between devices, fetch(): return lax.ppermute(array, chan, [(f, c) for c, f in source.items()])  7.22 us
    ppermute x3, waiting for transfers between devices, fetch(): return lax.ppermute(array, chan, [(f, c) for c, f in source.items()])  6.6 us
    pallas_call x1, Pallas kernels, whiten(): pl.pallas_call(whiten_kernel, in_specs=[pl.BlockSpec(memory_space=pltpu.H...  2.69 us
    pallas_call x1, Pallas kernels, stack(): pl.pallas_call(stack_kernel, in_specs=[whole] * 7, out_specs=pl.BlockSpec...  2.43 us
  transfers between devices with their start and end apart: 3, of which 3 were waited for; matrix products, arithmetic and copies ran while one was open for 0% of the time, Pallas kernels for 3%

profile of v6, /device:TPU:6, one launch (start us, length us, event | category | flops | bytes accessed | tf_op | source)
XLA Modules:
  0.0 32.2 jit_solution(8532697743731190498)
XLA Ops:
  0.0 0.0 copy-start.1
  0.0 0.0 copy-start
  0.0 0.0 copy-start.3
  0.0 0.0 copy-start.2
  0.0 2.7 %shard_map.64 = bf16[8,2,32,128]{3,2,1,0:T(8,128)(2,1)S(1)} custom-call(bf16[8,64,3000]{2,1,0:T(8,128)(2,1)} %constant.34.clone.table_hbm, bf16[3,160,3000]{2,1,0:T(8,128)(2,1)} %records_hbm.1), custom_call_target="tpu_custom_call" | custom-call | tf_op jit(solution)/shard_map/pallas_call | solution.py:113
  2.7 12.3 %all_to_all.5 = bf16[16,32,128]{2,1,0:T(8,128)(2,1)S(1)} all-to-all(bf16[16,32,128]{2,1,0:T(8,128)(2,1)S(1)} %bitcast.7), channel_id=1, replica_groups=mesh['tm'=8,'pair'=16,'side'=2] {'tm','side'}, dimensions={0} | all-to-all | bytes 262144 | tf_op jit(solution)/shard_map/all_to_all | solution.py:305
  15.0 5.0 %collective-permute-start = (bf16[8,2,32,128]{3,2,1,0:T(8,128)(2,1)S(1)}, bf16[8,2,32,128]{3,2,1,0:T(8,128)(2,1)S(1)}, u32[]{:S(2)}, u32[]{:S(2)}) collective-permute-start(bf16[8,2,32,128]{3,2,1,0:T(8,128)(2,1)S(1)} %bitcast.4), channel_id=1, source_target_pairs={{1,0},{2,1},{0,2},{4,3},{3,4},{6,5},{5,6},{8,7},{7,8},{10,9},{9,10... | collective-permute-start | bytes 393224 | tf_op jit(solution)/shard_map/ppermute | solution.py:302
  20.1 0.0 copy-done.1
  20.1 0.4 %shard_map.66 = (bf16[4,2,4,64,256]{4,3,2,1,0:T(8,128)(2,1)S(1)}, bf16[8,32,128]{2,1,0:T(8,128)(2,1)S(1)}) custom-call(s32[1]{0:T(128)} %bitcast.2.odd_ref, bf16[8,2,32,128]{3,2,1,0:T(8,128)(2,1)S(1)} %bitcast.5, bf16[4,128,256]{2,1,0:T(8,128)(2,1)S(1)} %copy-done.1), custom_call_target="tpu_custom_call" | custom-call | flops 70000000 | bytes 3000000 | tf_op jit(solution)/shard_map/pallas_call | solution.py:154
  20.4 2.2 %collective-permute-start.2 = (bf16[8,32,128]{2,1,0:T(8,128)(2,1)S(1)}, bf16[8,32,128]{2,1,0:T(8,128)(2,1)S(1)}, u32[]{:S(2)}, u32[]{:S(2)}) collective-permute-start(bf16[8,32,128]{2,1,0:T(8,128)(2,1)S(1)} %get-tuple-element.11), channel_id=1, source_target_pairs={{2,0},{4,1},{0,2},{6,3},{1,4},{8,5},{3,6},{10,7},{5,8},{12,9},{7,1... | collective-permute-start | bytes 196616 | tf_op jit(solution)/shard_map/ppermute | solution.py:302
  22.6 2.2 %collective-permute-done.near_ref = bf16[8,2,32,128]{3,2,1,0:T(8,128)(2,1)S(1)} collective-permute-done((bf16[8,2,32,128]{3,2,1,0:T(8,128)(2,1)S(1)}, bf16[8,2,32,128]{3,2,1,0:T(8,128)(2,1)S(1)}, u32[]{:S(2)}, u32[]{:S(2)}) %collective-permute-start) | collective-permute-done | bytes 131104 | tf_op jit(solution)/shard_map/ppermute | solution.py:302
  24.9 0.0 collective-permute-start.1
  24.9 0.0 copy-done.3
  24.9 0.0 copy-done
  24.9 0.0 copy-done.2
  24.9 0.6 %shard_map.65 = (bf16[4,2,160,512]{3,2,1,0:T(8,128)(2,1)S(1)}, f32[1,1280]{1,0:T(1,128)S(1)}) custom-call(s32[1,7]{1,0:T(1,128)S(1)} %copy-done.2, bf16[8,2,32,128]{3,2,1,0:T(8,128)(2,1)S(1)} %collective-permute-done.near_ref, bf16[8,2,32,128]{3,2,1,0:T(8,128)(2,1)S(1)} %bitcast.6, bf16[2,256,512]{2,1,0:T(8,128)(2,1)S(1)} %copy-done), custom_call_target="tpu_custom_call" | custom-call | flops 200000000 | bytes 3000000 | tf_op jit(solution)/shard_map/pallas_call | solution.py:198
  25.5 3.5 %collective-permute-done.2.edge_ref = bf16[8,32,128]{2,1,0:T(8,128)(2,1)S(1)} collective-permute-done((bf16[8,32,128]{2,1,0:T(8,128)(2,1)S(1)}, bf16[8,32,128]{2,1,0:T(8,128)(2,1)S(1)}, u32[]{:S(2)}, u32[]{:S(2)}) %collective-permute-start.2) | collective-permute-done | bytes 65568 | tf_op jit(solution)/shard_map/ppermute | solution.py:302
  28.9 0.9 %collective-permute-done.1.far_ref = bf16[8,2,32,128]{3,2,1,0:T(8,128)(2,1)S(1)} collective-permute-done((bf16[8,2,32,128]{3,2,1,0:T(8,128)(2,1)S(1)}, bf16[8,2,32,128]{3,2,1,0:T(8,128)(2,1)S(1)}, u32[]{:S(2)}, u32[]{:S(2)}) %collective-permute-start.1) | collective-permute-done | bytes 131104 | tf_op jit(solution)/shard_map/ppermute | solution.py:302
  29.8 2.4 %shard_map.67 = bf16[2,4,160,1120]{3,2,1,0:T(8,128)(2,1)} custom-call(s32[1,7]{1,0:T(1,128)S(1)} %broadcast_select_fusion.places_ref, f32[1,1280]{1,0:T(1,128)S(1)} %get-tuple-element.9.weight_ref, bf16[4,2,160,512]{3,2,1,0:T(8,128)(2,1)S(1)} %get-tuple-element.10.ready_ref, bf16[8,2,32,128]{3,2,1,0:T(8,128)(2,1)S(1)} %collective-permute-done.1.far_ref, ...), custom_call_target="tpu_custom_call" | custom-call | tf_op jit(solution)/shard_map/pallas_call | solution.py:262
  (1 shorter events, 0.0 us)
Async XLA Ops:
  0.0 20.1 %copy-start.1 = (bf16[4,128,256]{2,1,0:T(8,128)(2,1)S(1)}, bf16[4,128,256]{2,1,0:T(8,128)(2,1)}, u32[]{:S(2)}) copy-start(bf16[4,128,256]{2,1,0:T(8,128)(2,1)} %constant.36.clone.own_ref) | copy-start | bytes 786436
  0.0 24.9 %copy-start = (bf16[2,256,512]{2,1,0:T(8,128)(2,1)S(1)}, bf16[2,256,512]{2,1,0:T(8,128)(2,1)}, u32[]{:S(2)}) copy-start(bf16[2,256,512]{2,1,0:T(8,128)(2,1)} %constant.35.clone.gather_ref) | copy-start | bytes 1572868
  0.0 24.9 %copy-start.3 = (s32[1,7]{1,0:T(1,128)S(1)}, s32[1,7]{1,0:T(1,128)}, u32[]{:S(2)}) copy-start(s32[1,7]{1,0:T(1,128)} %param.7) | copy-start | bytes 88
  0.0 24.9 %copy-start.2 = (s32[1,7]{1,0:T(1,128)S(1)}, s32[1,7]{1,0:T(1,128)}, u32[]{:S(2)}) copy-start(s32[1,7]{1,0:T(1,128)} %valid_ref.1) | copy-start | bytes 88
  15.0 9.8 %collective-permute-start = (bf16[8,2,32,128]{3,2,1,0:T(8,128)(2,1)S(1)}, bf16[8,2,32,128]{3,2,1,0:T(8,128)(2,1)S(1)}, u32[]{:S(2)}, u32[]{:S(2)}) collective-permute-start(bf16[8,2,32,128]{3,2,1,0:T(8,128)(2,1)S(1)} %bitcast.4), channel_id=1, source_target_pairs={{1,0},{2,1},{0,2},{4,3},{3,4},{6,5},{5,6},{8,7},{7,8},{10,9},{9,10... | collective-permute-start | bytes 393224 | tf_op jit(solution)/shard_map/ppermute | solution.py:302
  20.4 8.5 %collective-permute-start.2 = (bf16[8,32,128]{2,1,0:T(8,128)(2,1)S(1)}, bf16[8,32,128]{2,1,0:T(8,128)(2,1)S(1)}, u32[]{:S(2)}, u32[]{:S(2)}) collective-permute-start(bf16[8,32,128]{2,1,0:T(8,128)(2,1)S(1)} %get-tuple-element.11), channel_id=1, source_target_pairs={{2,0},{4,1},{0,2},{6,3},{1,4},{8,5},{3,6},{10,7},{5,8},{12,9},{7,1... | collective-permute-start | bytes 196616 | tf_op jit(solution)/shard_map/ppermute | solution.py:302
  24.9 5.0 %collective-permute-start.1 = (bf16[8,2,32,128]{3,2,1,0:T(8,128)(2,1)S(1)}, bf16[8,2,32,128]{3,2,1,0:T(8,128)(2,1)S(1)}, u32[]{:S(2)}, u32[]{:S(2)}) collective-permute-start(bf16[8,2,32,128]{3,2,1,0:T(8,128)(2,1)S(1)} %collective-permute-done.near_ref), channel_id=1, source_target_pairs={{1,0},{0,1},{3,2},{2,3},{5,4},{4,5},{7,6},{6,7},{9,8},{8,9},{11,10... | collective-permute-start | bytes 393224 | tf_op jit(solution)/shard_map/ppermute | solution.py:302
